TPU v7x, 32 devices: a whole 2x2x4 slice. The times are simulated.
32 devices in a mesh: gx: 4 (over z), gy: 8 (over y, x, core).
Axes of the slice: x: 2, y: 2, z: 4, core: 2. Of those that a mesh axis runs over, the one named last changes fastest.
Arguments:
- leaf_up: float32 [96, 128, 456], P('gx', 'gy'), may hold values from -6 to 6
- parent_in: float32 [48, 64, 456], P('gx', 'gy'), may hold values from -6 to 6
- leaf_lists: int32 [96, 128, 40], P('gx', 'gy'), may hold values from 0 to 1, as said below
- parent_lists: int32 [48, 64, 40], P('gx', 'gy'), may hold values from 0 to 1, as said below
- up_transfer: float32 [4, 456, 456], replicated, may hold values from -0.125 to 0.125
- down_transfer: float32 [4, 456, 456], replicated, may hold values from -0.25 to 0.25
- check_inverse: float32 [456, 456], replicated, may hold values from -0.25 to 0.25
Outputs:
- leaf_down: float32 [96, 128, 456], P('gx', 'gy')
- parent_up: float32 [48, 64, 456], P('gx', 'gy')
Inputs may be any that keep to these rules, and one draw needn't show every extreme that they name: `leaf_lists`: A flag is 1 only where the box at that offset lies in the grid, its parent touches or equals the box's parent, and it holds surface points. `parent_lists`: A flag is 1 only where the parent at that offset lies in the grid, its parent touches or equals the box's parent, and it holds surface points.
All inputs are finite; a program needn't handle non-finite values.
Results may differ from a plain program's by a relative error of at most 0.0001.
Values sent between devices are 32-bit elements; how exact they have to be, the bound alone decides.
No kernel may reach another device: no remote copies, remote signals or barrier semaphores. Data moves between devices by JAX's collectives and lax.ppermute only.
A program may use at most 64 MiB of HBM per device.

v0:
```python
import functools
import math

import jax
import jax.numpy as jnp
import ml_dtypes
import numpy as np
from jax import lax
from jax.experimental import pallas as pl
from jax.experimental.pallas import tpu as pltpu
from jax.sharding import PartitionSpec as P

ORDER = 6
HALO = 4
KEPT = 14
BF16, F32 = jnp.bfloat16, jnp.float32

def offset_table():
    return [(a, b) for a in range(-3, 4) for b in range(-3, 4) if max(abs(a), abs(b)) >= 2]


BASES = sorted({(abs(a), abs(b)) for a, b in offset_table()})


def surface_points():
    grid = np.linspace(-1.0, 1.0, ORDER)
    keys = [
        (i, j, k)
        for i in range(ORDER)
        for j in range(ORDER)
        for k in range(ORDER)
        if min(i, j, k) == 0 or max(i, j, k) == ORDER - 1
    ]
    return keys, np.array([[grid[i] for i in key] for key in keys])


def translation(points, dx, dy):
    r = 0.525 * (points[:, None, :] - points[None, :, :]) - np.array([dx, dy, 0.0])
    dist = np.sqrt((r * r).sum(-1))
    n = len(points)
    out = np.zeros((3, n, 3, n))
    for a in range(3):
        for b in range(3):
            out[a, :, b, :] = (float(a == b) / dist + r[..., a] * r[..., b] / dist**3) / (8 * math.pi)
    return out.reshape(3 * n, 3 * n)


def split(x):
    high = x.astype(ml_dtypes.bfloat16)
    return high, (x - high.astype(np.float64)).astype(ml_dtypes.bfloat16)


@functools.lru_cache(maxsize=None)
def operators():
    keys, points = surface_points()
    n = len(keys)
    points_of = {key: i for i, key in enumerate(keys)}
    mirror = [points_of[(i, j, ORDER - 1 - k)] for i, j, k in keys]
    mats = {o: translation(points, *o) for o in offset_table()}
    half = 3 * n // 2
    rotation = np.zeros((3 * n, 512), ml_dtypes.bfloat16)
    back = np.zeros((512, 3 * n))
    table = np.zeros((2, len(BASES), 256, 256), ml_dtypes.bfloat16)
    signs = np.ones((4, 2, 256, 256), ml_dtypes.bfloat16)
    for s, sign in enumerate((1, -1)):
        pairs = np.zeros((3 * n, half))
        firsts = []
        for a in range(3):
            flip = sign if a < 2 else -sign
            for i in range(n):
                if i < mirror[i]:
                    pairs[a * n + i, len(firsts)] = 1.0
                    pairs[a * n + mirror[i], len(firsts)] = flip
                    firsts.append(a * n + i)
        blocks = {o: 0.25 * pairs.T @ m @ pairs for o, m in mats.items()}
        gram = sum(b.T @ b for b in blocks.values())
        place = {f: i for i, f in enumerate(firsts)}
        modes, parity, weight = [], [], []
        for sx in (1, -1):
            for sy in (1, -1):
                basis = []
                for i, f in enumerate(firsts):
                    a, (kx, ky, kz) = f // n, keys[f % n]
                    if kx < ORDER // 2 and ky < ORDER // 2:
                        v = np.zeros(half)
                        for fx in range(2):
                            for fy in range(2):
                                key = (ORDER - 1 - kx if fx else kx, ORDER - 1 - ky if fy else ky, kz)
                                sign_x = (sx if a != 0 else -sx) if fx else 1
                                sign_y = (sy if a != 1 else -sy) if fy else 1
                                v[place[a * n + points_of[key]]] = 0.5 * sign_x * sign_y
                        basis.append(v)
                basis = np.array(basis).T
                w, vecs = np.linalg.eigh(basis.T @ gram @ basis)
                vecs = basis @ vecs
                vecs = vecs * np.sign(vecs[np.abs(np.round(vecs, 9)).argmax(0), np.arange(len(w))])
                modes.append(vecs)
                weight.append(w)
                parity += [(sx, sy)] * len(w)
        order = np.argsort(-np.concatenate(weight), kind="stable")
        vecs = np.concatenate(modes, axis=1)[:, order]
        parity = np.array(parity)[order]
        modes = (pairs @ vecs / math.sqrt(2.0)).astype(ml_dtypes.bfloat16)
        lows = np.concatenate([modes, modes[:, :KEPT], modes[:, :KEPT]], axis=1)
        rotation[:, 256 * s : 256 * (s + 1)] = lows
        outs, out_parity = [], []
        for sx in (1, -1):
            for sy in (1, -1):
                for f in firsts:
                    a, (kx, ky, kz) = f // n, keys[f % n]
                    if kx < ORDER // 2 and ky < ORDER // 2:
                        v = np.zeros(half)
                        for fx in range(2):
                            for fy in range(2):
                                key = (ORDER - 1 - kx if fx else kx, ORDER - 1 - ky if fy else ky, kz)
                                sign_x = (sx if a != 0 else -sx) if fx else 1
                                sign_y = (sy if a != 1 else -sy) if fy else 1
                                v[place[a * n + points_of[key]]] = sign_x * sign_y
                        outs.append(v)
                        out_parity.append((sx, sy))
        outs = np.array(outs).T
        out_parity = np.array(out_parity)
        back[256 * s : 256 * s + half] = (pairs @ outs).T
        undo = np.linalg.inv(modes[firsts].astype(np.float64))
        for q, o in enumerate(BASES):
            high, low = split(undo @ blocks[o].T @ outs * 0.25)
            table[s, q, :half, :half] = high
            table[s, q, half : half + KEPT, :half] = high[:KEPT]
            table[s, q, half + KEPT : half + 2 * KEPT, :half] = low[:KEPT]
        ins = np.concatenate([parity, parity[:KEPT], parity[:KEPT]], axis=0)
        for f in range(4):
            row = np.ones(256)
            row[: len(ins)] = (ins[:, 0] if f // 2 else 1) * (ins[:, 1] if f % 2 else 1)
            col = np.ones(256)
            col[:half] = (out_parity[:, 0] if f // 2 else 1) * (out_parity[:, 1] if f % 2 else 1)
            signs[f, s] = row[:, None] * col[None, :]
    whole = [
        table[:, BASES.index((abs(a), abs(b)))] * signs[2 * (a < 0) + (b < 0)]
        for a, b in offset_table()
    ]
    return rotation, back.astype(ml_dtypes.bfloat16), np.stack(whole, axis=1)


@functools.lru_cache(maxsize=None)
def plan():
    products = []
    for c, d in class_pairs():
        for o, (dx, dy) in enumerate(offset_table()):
            px, cs = divmod(c + dx, 2)
            py, ds = divmod(d + dy, 2)
            if abs(px) <= 1 and abs(py) <= 1:
                products.append((o, (cs * 3 + px + 1) * 6 + ds * 3 + py + 1))
    return products


def class_pairs():
    return [(c, d) for c in range(2) for d in range(2)]


def dot(a, b):
    return lax.dot_general(a, b, (((1,), (0,)), ((), ())), preferred_element_type=F32)


def dot_t(a, b):
    return lax.dot_general(a, b, (((1,), (1,)), ((), ())), preferred_element_type=F32)


def parts(x):
    high = x.astype(BF16)
    return high, (x - high.astype(F32)).astype(BF16)


def times_t(x, weight):
    xh, xl = parts(x)
    wh, wl = weight
    both = dot_t(jnp.concatenate([xh, xl], axis=0), wh)
    return both[: x.shape[0]] + (both[x.shape[0] :] + dot_t(xh, wl))


def times_exact(x, weight):
    both = dot(jnp.concatenate(parts(x), axis=0), weight)
    return both[: x.shape[0]] + both[x.shape[0] :]


def lanes(ref, *at):
    pieces = [ref[(t,) + at] for t in range(4)]
    pieces = [p.reshape(-1, 128) for p in pieces]
    return jnp.concatenate(pieces, axis=1)


def cut_tiles(dens):
    return [(t, slice(128 * t, min(128 * t + 128, dens)), slice(0, min(128, dens - 128 * t))) for t in range(4)]


def modes_of(x, rot_ref, dens):
    y = times_exact(x[:, :dens], rot_ref[...])
    lane = lax.broadcasted_iota(jnp.int32, (1, 512), 1) % 256
    half = dens // 2
    is_low = (lane >= half) & (lane < half + KEPT)
    return jnp.where(is_low, y - y.astype(BF16).astype(F32), y)


def children(ref, dens, counts, c, d):
    return jnp.concatenate(
        [
            jnp.concatenate(
                [ref[t, 2 * i + c, pl.ds(d, counts[1], stride=2), :] for i in range(counts[0])],
                axis=0,
            )
            for t in range(4)
        ],
        axis=1,
    )[:, :dens]


def own_kernel(own_ref, rot_ref, modes_ref):
    rows, cols, dens = own_ref.shape
    y = modes_of(own_ref[...].reshape(rows * cols, dens), rot_ref, dens)
    for t in range(4):
        modes_ref[t] = y[:, 128 * t : 128 * t + 128].reshape(rows, cols, 128)


def near_kernel(
    even_ref, strip0_ref, strip1_ref, own_ref, own_modes_ref, rot_ref, up_ref, llist_ref, plist_ref,
    pup_ref, lut, edge_ref, pmodes_ref, masks_ref, upw_ref,
    own_t, strip_t, modes, flat,
):
    rows, cols, dens = own_ref.shape
    pr, pc = rows // 2, cols // 2
    gr, gc = pr // 2, pc // 2
    boxes = pr * pc
    used = boxes + gr * gc
    high = lut.shape[2]
    count = masks_ref.shape[0] // 4
    even = even_ref[1] == 1
    for t, cut, to in cut_tiles(dens):
        own_t[t, :, :, to] = own_ref[:, :, cut]
        first, second = strip0_ref[:, :, cut], strip1_ref[:, :, cut]
        strip_t[t, :, 0:HALO, to] = jnp.where(even, second, first)
        strip_t[t, :, HALO:, to] = jnp.where(even, first, second)

    parent = None
    for n, (c, d) in enumerate(class_pairs()):
        upw_ref[n, 0], upw_ref[n, 1] = parts(up_ref[n])
        x = jnp.concatenate(
            [children(own_t, dens, (pr, pc), c, d), children(strip_t, dens, (pr, HALO), c, d)],
            axis=0,
        )
        part = times_t(x, (upw_ref[n, 0], upw_ref[n, 1]))
        parent = part if parent is None else parent + part
    pup_ref[...] = parent[:boxes].reshape(pr, pc, dens)
    z = modes_of(jnp.concatenate([lanes(strip_t)[:, :dens], parent], axis=0), rot_ref, dens)
    w, p = z[: rows * 8], z[rows * 8 :]
    for t in range(4):
        cut = slice(128 * t, 128 * t + 128)
        modes[t, 2 : 2 + rows, 8 : 8 + cols, :] = own_modes_ref[t]
        strip = w[:, cut].reshape(rows, 8, 128)
        modes[t, 2 : 2 + rows, 4:8, :] = strip[:, 0:4]
        modes[t, 2 : 2 + rows, 8 + cols : 12 + cols, :] = strip[:, 4:8]
        edge_ref[t, 0:2] = modes[t, 2:4]
        edge_ref[t, 2:4] = modes[t, rows : rows + 2]
        pmodes_ref[t, 2 : 2 + pr, 4 : 4 + pc, :] = p[:boxes, cut].reshape(pr, pc, 128)
        strip = p[boxes:, cut].reshape(pr, 4, 128)
        pmodes_ref[t, 2 : 2 + pr, 2:4, :] = strip[:, 0:2]
        pmodes_ref[t, 2 : 2 + pr, 4 + pc : 6 + pc, :] = strip[:, 2:4]

    def gather(i, carry):
        base = 2 * (i % 3) + i // 3
        for ds in range(2):
            for py in (-1, 0, 1):
                e = i * 6 + ds * 3 + py + 1
                for t in range(4):
                    x = jnp.concatenate(
                        [
                            modes[t, base + 2 * j, pl.ds(8 + 2 * py + ds, pc, stride=2), :]
                            for j in range(pr)
                        ]
                        + [
                            pmodes_ref[t, base + 2 * j, pl.ds(4 + 2 * py + ds, gc, stride=2), :]
                            for j in range(gr)
                        ]
                        + [jnp.zeros((high - used, 128), F32)],
                        axis=0,
                    )
                    lut[e, t // 2, :, 128 * (t % 2) : 128 * (t % 2) + 128] = x.astype(BF16)
        return carry

    lax.fori_loop(0, 6, gather, 0)

    flat[0, :, :, 0 : llist_ref.shape[2]] = llist_ref[...].astype(F32)
    flat[1, 0:pr, 0:pc, 0 : plist_ref.shape[2]] = plist_ref[...].astype(F32)
    for n, (c, d) in enumerate(class_pairs()):
        flag = jnp.concatenate(
            [flat[0, 2 * i + c, pl.ds(d, pc, stride=2), :] for i in range(pr)]
            + [flat[1, 2 * i + c, pl.ds(d, gc, stride=2), :] for i in range(gr)]
            + [jnp.zeros((high - used, 128), F32)],
            axis=0,
        )
        for k in range(count):
            o = plan()[count * n + k][0]
            masks_ref[count * n + k] = jnp.broadcast_to(flag[:, o : o + 1], (high, 128)).astype(BF16)


def close_kernel(
    entry_ref, pick_ref, even_ref,
    end0_ref, end1_ref, edge_ref, pside_ref, upw_ref, masks, lut_ref,
    rot_ref, pin_ref, back, table, down_ref, inv_ref,
    out_ref,
    ends_t, edge, pmodes, lut, acc, flat, plocal, sem,
):
    rows, cols, dens = out_ref.shape
    pr, pc = rows // 2, cols // 2
    gr, gc = pr // 2, pc // 2
    boxes, pboxes = pr * pc, gr * gc
    high = lut.shape[2]
    wide = end0_ref.shape[1]
    count = masks.shape[0] // 4
    copy = pltpu.make_async_copy(lut_ref, lut, sem)
    copy.start()
    even = even_ref[0] == 1
    for t, cut, to in cut_tiles(dens):
        first, second = end0_ref[:, :, cut], end1_ref[:, :, cut]
        ends_t[t, 0:HALO, :, to] = jnp.where(even, second, first)
        ends_t[t, HALO:, :, to] = jnp.where(even, first, second)
    parent = None
    for n, (c, d) in enumerate(class_pairs()):
        x = children(ends_t, dens, (HALO, wide // 2), c, d)
        part = times_t(x, (upw_ref[n, 0], upw_ref[n, 1]))
        parent = part if parent is None else parent + part
    x = lanes(ends_t, slice(HALO - 2, HALO + 2))[:, :dens]
    y = modes_of(jnp.concatenate([x, parent], axis=0), rot_ref, dens)
    z, p = y[: 4 * wide], y[4 * wide :]
    for t in range(4):
        cut = slice(128 * t, 128 * t + 128)
        end = z[:, cut].reshape(4, wide, 128)
        edge[t, 0:2, 4 : 4 + wide, :] = end[0:2]
        edge[t, 2:4] = edge_ref[t, 0:2]
        edge[t, 4:6] = edge_ref[t, 2:4]
        edge[t, 6:8, 4 : 4 + wide, :] = end[2:4]
        end = p[:, cut].reshape(4, wide // 2, 128)
        pmodes[t, 0:2, 2 : 2 + wide // 2, :] = end[0:2]
        pmodes[t, 2 : 2 + pr] = pside_ref[t, 2 : 2 + pr]
        pmodes[t, 2 + pr :, 2 : 2 + wide // 2, :] = end[2:4]

    copy.wait()

    def patch(cs, carry):
        for ds in range(2):
            for py in (-1, 0, 1):
                for t in range(4):
                    at = slice(128 * (t % 2), 128 * (t % 2) + 128)
                    mine = pl.ds(8 + 2 * py + ds, pc, stride=2)
                    theirs = pl.ds(4 + 2 * py + ds, gc, stride=2)
                    e = cs * 18 + ds * 3 + py + 1
                    x = jnp.concatenate([edge[t, cs + 2 * j, mine, :] for j in range(2)], axis=0)
                    lut[e, t // 2, 0:16, at] = x.astype(BF16)
                    x = jnp.concatenate([pmodes[t, cs + 2 * j, theirs, :] for j in range(4)], axis=0)
                    lut[e, t // 2, boxes : boxes + 16, at] = x.astype(BF16)
                    e = e + 12
                    x = jnp.concatenate([edge[t, 4 + cs + 2 * j, mine, :] for j in range(2)], axis=0)
                    lut[e, t // 2, boxes - 16 : boxes, at] = x.astype(BF16)
                    x = jnp.concatenate(
                        [pmodes[t, 4 + cs + 2 * j, theirs, :] for j in range(4, gr)]
                        + [jnp.zeros((high - boxes - pboxes, 128), F32)],
                        axis=0,
                    )
                    lut[e, t // 2, boxes + 16 : high, at] = x.astype(BF16)
        return carry

    lax.fori_loop(0, 2, patch, 0)

    def interact(j, carry):
        n, s = j // 2, j % 2
        total = jnp.zeros((high, 256), F32)
        for k in range(count):
            i = n * count + k
            m = masks[i]
            x = lut[entry_ref[i], s]
            x = jnp.concatenate([x[:, :128] * m, x[:, 128:] * m], axis=1)
            total = total + dot(x, table[s, pick_ref[i]])
        acc[s, n] = total
        return carry

    lax.fori_loop(0, 8, interact, 0)

    check = None
    for s in range(2):
        part = times_exact(acc[s].reshape(4 * high, 256), back[256 * s : 256 * (s + 1)])
        check = part if check is None else check + part

    inverse = parts(inv_ref[...])
    for n, (c, d) in enumerate(class_pairs()):
        for t, cut, to in cut_tiles(dens):
            for j in range(gr):
                r = high * n + boxes + gc * j
                plocal[t, 2 * j + c, pl.ds(d, gc, stride=2), to] = check[r : r + gc, cut]
    local = pin_ref[...].reshape(boxes, dens) + times_t(lanes(plocal)[:, :dens], inverse)
    x = jnp.concatenate(
        [
            check[high * n : high * n + boxes] + times_t(local, parts(down_ref[n]))
            for n in range(4)
        ],
        axis=0,
    )
    result = times_t(x, inverse)
    for n, (c, d) in enumerate(class_pairs()):
        for t, cut, to in cut_tiles(dens):
            for j in range(pr):
                r = boxes * n + pc * j
                flat[t, 2 * j + c, pl.ds(d, pc, stride=2), to] = result[r : r + pc, cut]
    for t, cut, to in cut_tiles(dens):
        out_ref[:, :, cut] = flat[t, :, :, to]


VMEM = pl.BlockSpec(memory_space=pltpu.VMEM)
SMEM = pl.BlockSpec(memory_space=pltpu.SMEM)


def params(mib):
    return pltpu.CompilerParams(vmem_limit_bytes=mib * 1024 * 1024)


def cost(rows, tiles, reads):
    return pl.CostEstimate(flops=2 * rows * tiles * 256 * 256, bytes_accessed=reads, transcendentals=0)


def height(boxes):
    return -(-(boxes * 5 // 4) // 16) * 16


def own_step(own, rotation):
    rows, cols, _ = own.shape
    return pl.pallas_call(
        own_kernel,
        out_shape=jax.ShapeDtypeStruct((4, rows, cols, 128), F32),
        in_specs=[VMEM] * 2,
        out_specs=VMEM,
        compiler_params=params(16),
        cost_estimate=cost(rows * cols, 48, 16 * 1024 * 1024),
    )(own, rotation)


def near_step(even, strips, own, own_modes, rotation, up, llist, plist):
    rows, cols, dens = own.shape
    pr, pc = rows // 2, cols // 2
    high = height(pr * pc)
    return pl.pallas_call(
        near_kernel,
        out_shape=(
            jax.ShapeDtypeStruct((pr, pc, dens), F32),
            jax.ShapeDtypeStruct((36, 2, high, 256), BF16),
            jax.ShapeDtypeStruct((4, 4, cols + 16, 128), F32),
            jax.ShapeDtypeStruct((4, pr + 4, pc + 8, 128), F32),
            jax.ShapeDtypeStruct((len(plan()), high, 128), BF16),
            jax.ShapeDtypeStruct((4, 2, dens, dens), BF16),
        ),
        in_specs=[SMEM] + [VMEM] * 8,
        out_specs=(VMEM,) * 6,
        scratch_shapes=[
            pltpu.VMEM((4, rows, cols, 128), F32),
            pltpu.VMEM((4, rows, 2 * HALO, 128), F32),
            pltpu.VMEM((4, rows + 4, cols + 16, 128), F32),
            pltpu.VMEM((2, rows, cols, 128), F32),
        ],
        compiler_params=params(24),
        cost_estimate=cost(rows * cols, 48, up.size * 4),
    )(even, *strips, own, own_modes, rotation, up, llist, plist)


def close_step(even, ends, edge, pmodes, upw, masks, lut, rotation, pin, back, table, down, inv, shape):
    rows, cols, dens = shape
    pr, pc = rows // 2, cols // 2
    high = height(pr * pc)
    return pl.pallas_call(
        close_kernel,
        out_shape=jax.ShapeDtypeStruct(shape, F32),
        in_specs=[SMEM] * 3 + [VMEM] * 13,
        out_specs=VMEM,
        scratch_shapes=[
            pltpu.VMEM((4, 2 * HALO, cols + 2 * HALO, 128), F32),
            pltpu.VMEM((4, 8, cols + 16, 128), F32),
            pltpu.VMEM((4, pr + 4, pc + 8, 128), F32),
            pltpu.VMEM(lut.shape, BF16),
            pltpu.VMEM((2, 4, high, 256), F32),
            pltpu.VMEM((4, rows, cols, 128), F32),
            pltpu.VMEM((4, pr, pc, 128), F32),
            pltpu.SemaphoreType.DMA,
        ],
        compiler_params=params(24),
        cost_estimate=cost(rows * cols, 150, table.size * 2),
    )(
        jnp.asarray([e for _, e in plan()], jnp.int32), jnp.asarray([o for o, _ in plan()], jnp.int32),
        even, *ends, edge, pmodes, upw, masks, lut, rotation, pin, back, table, down, inv,
    )


def swapped(low, high, axis, odd_first):
    peers = lax.axis_size(axis)
    even = lax.axis_index(axis) % 2 == 0
    strips = (jnp.where(even, high, low), jnp.where(even, low, high))
    got = [None, None]
    for kind in (1, 0) if odd_first else (0, 1):
        pairs = [(i, i + 1) for i in range(kind, peers - 1, 2)]
        got[kind] = lax.ppermute(strips[kind], axis, pairs + [(j, i) for i, j in pairs])
    return got


def local(leaf_up, parent_in, leaf_lists, parent_lists, up_transfer, down_transfer, check_inverse):
    rows, cols, _ = leaf_up.shape
    even = [lax.axis_index(axis) % 2 == 0 for axis in ("gx", "gy")]
    flag = jnp.stack(even).astype(jnp.int32)
    rotation, back, table = (jnp.asarray(x) for x in operators())
    strips = swapped(leaf_up[:, :HALO], leaf_up[:, cols - HALO :], "gy", True)
    *strips, own_modes = lax.optimization_barrier((*strips, own_step(leaf_up, rotation)))
    left = jnp.where(even[1], strips[1], strips[0])
    right = jnp.where(even[1], strips[0], strips[1])
    broad = lambda s: jnp.concatenate([left[s], leaf_up[s], right[s]], axis=1)
    ends = swapped(broad(slice(0, HALO)), broad(slice(rows - HALO, rows)), "gx", False)
    parent_up, lut, edge, pmodes, masks, upw = near_step(
        flag, strips, leaf_up, own_modes, rotation, up_transfer, leaf_lists, parent_lists
    )
    leaf_down = close_step(
        flag, ends, edge, pmodes, upw, masks, lut, rotation, parent_in, back, table,
        down_transfer, check_inverse, leaf_up.shape,
    )
    return leaf_down, parent_up


def solution(mesh):
    block = P("gx", "gy", None)
    return jax.shard_map(
        local,
        mesh=mesh,
        in_specs=(block,) * 4 + (P(),) * 3,
        out_specs=(block, block),
        check_vma=False,
    )
```

profile of v0, /device:TPU:12, one launch (start us, length us, event | category | flops | bytes accessed | tf_op | source)
XLA Modules:
  0.0 37.7 jit_solution(10215625964301671598)
XLA Ops:
  0.6 1.2 %slice_select_fusion = (f32[24,4,456]{2,1,0:T(4,128)S(1)}, f32[24,4,456]{2,1,0:T(4,128)S(1)}) fusion(f32[24,16,456]{2,1,0:T(8,128)} %own_ref.3, pred[]{:T(512)} %eq.14), kind=kLoop, calls=%fused_computation.2 | loop fusion | flops 87552 | bytes 700417 | tf_op jit(solution)/shard_map/jit(_where)/select_n | solution.py:500
  1.8 0.1 collective-permute-start
  1.9 3.4 %collective-permute-start.1 = (f32[24,4,456]{2,1,0:T(4,128)S(1)}, f32[24,4,456]{2,1,0:T(4,128)S(1)}, u32[]{:S(2)}, u32[]{:S(2)}) collective-permute-start(f32[24,4,456]{2,1,0:T(4,128)S(1)} %get-tuple-element.22), channel_id=1, source_target_pairs={{1,2},{3,4},{5,6},{2,1},{4,3},{6,5},{9,10},{11,12},{13,14},{10,9},... | collective-permute-start | bytes 525320 | tf_op jit(solution)/shard_map/ppermute | solution.py:504
  5.4 1.0 %fusion.2 = (f32[4,16,456]{2,1,0:T(8,128)S(1)}, f32[4,16,456]{2,1,0:T(8,128)S(1)}) fusion(f32[24,16,456]{2,1,0:T(8,128)} %own_ref.3), kind=kLoop, calls=%fused_computation.9 | loop fusion | bytes 466944 | tf_op jit(solution)/shard_map/slice | solution.py:517
  6.4 0.1 add_convert_fusion.even_ref
  6.5 0.0 copy-start.2
  6.5 1.1 %copy-done.2 = f32[24,16,456]{2,1,0:T(8,128)S(1)} copy-done((f32[24,16,456]{2,1,0:T(8,128)S(1)}, f32[24,16,456]{2,1,0:T(8,128)}, u32[]{:S(2)}) %copy-start.2) | copy-done | bytes 700440
  7.6 0.0 copy-start.5
  7.6 1.0 %copy-done.5 = bf16[456,512]{1,0:T(8,128)(2,1)S(1)} copy-done((bf16[456,512]{1,0:T(8,128)(2,1)S(1)}, bf16[456,512]{1,0:T(8,128)(2,1)}, u32[]{:S(2)}) %copy-start.5) | copy-done | bytes 466968
  8.6 0.0 copy-start.3
  8.6 0.0 copy-start.6
  8.6 0.0 copy-start.11
  8.6 0.0 copy-start.12
  8.6 0.0 slice-start
  8.6 0.0 slice-start.1
  8.6 0.6 %shard_map.131.own_modes_ref = f32[4,24,16,128]{3,2,1,0:T(8,128)S(1)} custom-call(f32[24,16,456]{2,1,0:T(8,128)S(1)} %copy-done.2, bf16[456,512]{1,0:T(8,128)(2,1)S(1)} %copy-done.5), custom_call_target="tpu_custom_call" | custom-call | flops 2415919104 | bytes 16777216 | tf_op jit(solution)/shard_map/pallas_call | solution.py:433
  9.2 0.0 collective-permute-done.strip0_ref
  9.2 2.4 %collective-permute-done.1.strip1_ref = f32[24,4,456]{2,1,0:T(4,128)S(1)} collective-permute-done((f32[24,4,456]{2,1,0:T(4,128)S(1)}, f32[24,4,456]{2,1,0:T(4,128)S(1)}, u32[]{:S(2)}, u32[]{:S(2)}) %collective-permute-start.1) | collective-permute-done | bytes 175136 | tf_op jit(solution)/shard_map/ppermute | solution.py:504
  11.7 0.1 fusion
  11.8 0.1 collective-permute-start.2
  11.8 0.0 slice-start.2
  11.9 0.0 copy-start
  11.9 0.0 copy-start.1
  11.9 0.0 copy-start.4
  11.9 0.0 copy-start.7
  11.9 0.0 copy-start.8
  11.9 0.0 copy-start.9
  11.9 5.3 %collective-permute-start.3 = (f32[4,24,456]{2,1,0:T(8,128)S(1)}, f32[4,24,456]{2,1,0:T(8,128)S(1)}, u32[]{:S(2)}, u32[]{:S(2)}) collective-permute-start(f32[4,24,456]{2,1,0:T(8,128)S(1)} %get-tuple-element.24), channel_id=1, source_target_pairs={{8,16},{16,8},{9,17},{17,9},{10,18},{18,10},{11,19},{19,11},{12,20... | collective-permute-start | bytes 525320 | tf_op jit(solution)/shard_map/ppermute | solution.py:504
  17.2 0.0 copy-done.3
  17.2 0.0 copy-done.6
  17.2 0.0 copy-done.11
  17.2 0.0 copy-done.12
  17.3 0.0 copy-start.10
  17.3 2.0 %copy-done.10 = f32[4,456,456]{2,1,0:T(8,128)S(1)} copy-done((f32[4,456,456]{2,1,0:T(8,128)S(1)}, f32[4,456,456]{2,1,0:T(8,128)}, u32[]{:S(2)}) %copy-start.10) | copy-done | bytes 3327000
  19.3 5.4 %shard_map.132 = (f32[12,8,456]{2,1,0:T(8,128)}, bf16[36,2,128,256]{3,2,1,0:T(8,128)(2,1)S(1)}, f32[4,4,32,128]{3,2,1,0:T(8,128)S(1)}, f32[4,16,16,128]{3,2,1,0:...) custom-call(s32[2]{0:T(128)S(1)} %add_convert_fusion.even_ref, ...), custom_call_target="tpu_custom_call" | custom-call | flops 2415919104 | bytes 3326976 | tf_op jit(solution)/shard_map/pallas_call | solution.py:447
  24.8 0.0 collective-permute-done.2.end0_ref
  24.8 0.0 collective-permute-done.3.end1_ref
  24.8 0.0 slice-done
  24.8 0.0 slice-done.1
  24.8 0.0 slice-done.2
  24.8 0.0 copy-done
  24.8 0.0 copy-done.1
  24.8 0.0 copy-done.4
  24.8 0.0 copy-done.7
  24.8 0.0 copy-done.8
  24.9 0.0 copy-done.9
  24.9 12.8 %shard_map.133 = f32[24,16,456]{2,1,0:T(8,128)} custom-call(s32[108]{0:T(128)S(1)} %copy-done.8, s32[108]{0:T(128)S(1)} %copy-done.9, s32[2]{0:T(128)S(1)} %add_convert_fusion.even_ref, f32[4,24,456]{2,1,0:T(8,128)S(1)} %collective-permute-done.2.end0_ref, f32[4,24,456]{2,1,0:T(8,128)S(1)} %collective-permute-done.3.end1_ref, ...), custom_call_target="tpu_custom_call" | custom-call | flops 7549747200 | bytes 10485760 | tf_op jit(solution)/shard_map/pallas_call | solution.py:474
  (3 shorter events, 0.0 us)
Async XLA Ops:
  1.8 7.4 %collective-permute-start = (f32[24,4,456]{2,1,0:T(4,128)S(1)}, f32[24,4,456]{2,1,0:T(4,128)S(1)}, u32[]{:S(2)}, u32[]{:S(2)}) collective-permute-start(f32[24,4,456]{2,1,0:T(4,128)S(1)} %get-tuple-element.23), channel_id=1, source_target_pairs={{0,1},{2,3},{4,5},{6,7},{1,0},{3,2},{5,4},{7,6},{8,9},{10,11},{12,... | collective-permute-start | bytes 525320 | tf_op jit(solution)/shard_map/ppermute | solution.py:504
  1.9 9.7 %collective-permute-start.1 = (f32[24,4,456]{2,1,0:T(4,128)S(1)}, f32[24,4,456]{2,1,0:T(4,128)S(1)}, u32[]{:S(2)}, u32[]{:S(2)}) collective-permute-start(f32[24,4,456]{2,1,0:T(4,128)S(1)} %get-tuple-element.22), channel_id=1, source_target_pairs={{1,2},{3,4},{5,6},{2,1},{4,3},{6,5},{9,10},{11,12},{13,14},{10,9},... | collective-permute-start | bytes 525320 | tf_op jit(solution)/shard_map/ppermute | solution.py:504
  6.5 1.1 %copy-start.2 = (f32[24,16,456]{2,1,0:T(8,128)S(1)}, f32[24,16,456]{2,1,0:T(8,128)}, u32[]{:S(2)}) copy-start(f32[24,16,456]{2,1,0:T(8,128)} %own_ref.3) | copy-start | bytes 2101252
  7.6 1.0 %copy-start.5 = (bf16[456,512]{1,0:T(8,128)(2,1)S(1)}, bf16[456,512]{1,0:T(8,128)(2,1)}, u32[]{:S(2)}) copy-start(bf16[456,512]{1,0:T(8,128)(2,1)} %constant.40.clone.rot_ref) | copy-start | bytes 1400836
  8.6 8.6 %copy-start.3 = (f32[24,16,456]{2,1,0:T(8,128)S(1)}, f32[24,16,456]{2,1,0:T(8,128)}, u32[]{:S(2)}) copy-start(f32[24,16,456]{2,1,0:T(8,128)} %own_ref.3) | copy-start | bytes 2101252
  8.6 8.6 %copy-start.6 = (bf16[456,512]{1,0:T(8,128)(2,1)S(1)}, bf16[456,512]{1,0:T(8,128)(2,1)}, u32[]{:S(2)}) copy-start(bf16[456,512]{1,0:T(8,128)(2,1)} %constant.40.clone.rot_ref) | copy-start | bytes 1400836
  8.6 8.6 %copy-start.11 = (s32[24,16,40]{2,1,0:T(8,128)S(1)}, s32[24,16,40]{2,1,0:T(8,128)}, u32[]{:S(2)}) copy-start(s32[24,16,40]{2,1,0:T(8,128)} %llist_ref.1) | copy-start | bytes 184324
  8.6 8.6 %copy-start.12 = (s32[12,8,40]{2,1,0:T(8,128)S(1)}, s32[12,8,40]{2,1,0:T(8,128)}, u32[]{:S(2)}) copy-start(s32[12,8,40]{2,1,0:T(8,128)} %plist_ref.1) | copy-start | bytes 46084
  8.6 16.2 %slice-start = ((s8[10485760]{0:T(1024)(128)(4,1)}), s8[4194304]{0:T(1024)(128)(4,1)S(1)}, s32[]{:S(2)}) async-start(s8[10485760]{0:T(1024)(128)(4,1)} %bitcast.6), calls=%async_computation | async-start | bytes 8388608
  8.6 16.2 %slice-start.1 = ((s8[10485760]{0:T(1024)(128)(4,1)}), s8[4194304]{0:T(1024)(128)(4,1)S(1)}, s32[]{:S(2)}) async-start(s8[10485760]{0:T(1024)(128)(4,1)} %bitcast.6), calls=%async_computation.1 | async-start | bytes 8388608
  11.8 13.0 %collective-permute-start.2 = (f32[4,24,456]{2,1,0:T(8,128)S(1)}, f32[4,24,456]{2,1,0:T(8,128)S(1)}, u32[]{:S(2)}, u32[]{:S(2)}) collective-permute-start(f32[4,24,456]{2,1,0:T(8,128)S(1)} %get-tuple-element.25), channel_id=1, source_target_pairs={{0,8},{16,24},{8,0},{24,16},{1,9},{17,25},{9,1},{25,17},{2,10},{18... | collective-permute-start | bytes 525320 | tf_op jit(solution)/shard_map/ppermute | solution.py:504
  11.8 13.0 %slice-start.2 = ((s8[10485760]{0:T(1024)(128)(4,1)}), s8[2097152]{0:T(1024)(128)(4,1)S(1)}, s32[]{:S(2)}) async-start(s8[10485760]{0:T(1024)(128)(4,1)} %bitcast.6), calls=%async_computation.2 | async-start | bytes 4194304
  11.9 13.0 %copy-start = (f32[4,456,456]{2,1,0:T(8,128)S(1)}, f32[4,456,456]{2,1,0:T(8,128)}, u32[]{:S(2)}) copy-start(f32[4,456,456]{2,1,0:T(8,128)} %down_ref.1) | copy-start | bytes 9980932
  11.9 13.0 %copy-start.1 = (f32[456,456]{1,0:T(8,128)S(1)}, f32[456,456]{1,0:T(8,128)}, u32[]{:S(2)}) copy-start(f32[456,456]{1,0:T(8,128)} %inv_ref.1) | copy-start | bytes 2495236
  11.9 12.9 %copy-start.4 = (bf16[512,456]{1,0:T(8,128)(2,1)S(1)}, bf16[512,456]{1,0:T(8,128)(2,1)}, u32[]{:S(2)}) copy-start(bf16[512,456]{1,0:T(8,128)(2,1)} %constant.41.clone.back) | copy-start | bytes 1400836
  11.9 12.9 %copy-start.7 = (f32[12,8,456]{2,1,0:T(8,128)S(1)}, f32[12,8,456]{2,1,0:T(8,128)}, u32[]{:S(2)}) copy-start(f32[12,8,456]{2,1,0:T(8,128)} %pin_ref.1) | copy-start | bytes 525316
  11.9 12.9 %copy-start.8 = (s32[108]{0:T(128)S(1)}, s32[108]{0:T(128)}, u32[]{:S(2)}) copy-start(s32[108]{0:T(128)} %constant.43.clone.entry_ref) | copy-start | bytes 1300
  11.9 12.9 %copy-start.9 = (s32[108]{0:T(128)S(1)}, s32[108]{0:T(128)}, u32[]{:S(2)}) copy-start(s32[108]{0:T(128)} %constant.44.clone.pick_ref) | copy-start | bytes 1300
  11.9 12.8 %collective-permute-start.3 = (f32[4,24,456]{2,1,0:T(8,128)S(1)}, f32[4,24,456]{2,1,0:T(8,128)S(1)}, u32[]{:S(2)}, u32[]{:S(2)}) collective-permute-start(f32[4,24,456]{2,1,0:T(8,128)S(1)} %get-tuple-element.24), channel_id=1, source_target_pairs={{8,16},{16,8},{9,17},{17,9},{10,18},{18,10},{11,19},{19,11},{12,20... | collective-permute-start | bytes 525320 | tf_op jit(solution)/shard_map/ppermute | solution.py:504
  17.3 2.1 %copy-start.10 = (f32[4,456,456]{2,1,0:T(8,128)S(1)}, f32[4,456,456]{2,1,0:T(8,128)}, u32[]{:S(2)}) copy-start(f32[4,456,456]{2,1,0:T(8,128)} %up_ref.1) | copy-start | bytes 9980932
where the time goes:
time: 38 us; the launch traced here: 37.7 us
  Pallas kernels  18.8 us (49%)
  starting transfers between devices  8.85 us (23%)
  local copies, waits for them, and re-layouts  5.28 us (14%)
  waiting for transfers between devices  2.4 us (6%)
  other arithmetic  1.38 us (4%)
  between operations  0.96 us (3%)
    pallas_call x1, Pallas kernels, close_step(): pl.pallas_call(close_kernel, out_shape=jax.ShapeDtypeStruct(shape, F32),...  12.8 us
    ppermute x4, starting transfers between devices, swapped(): lax.ppermute(strips[kind], axis, pairs + [(j, i) for i, j in pairs])  8.85 us
    pallas_call x1, Pallas kernels, near_step(): pl.pallas_call(near_kernel, out_shape=(jax.ShapeDtypeStruct((pr, pc, dens...  5.44 us
    unnamed x32, local copies, waits for them, and re-layouts  4.28 us
    ppermute x4, waiting for transfers between devices, swapped(): lax.ppermute(strips[kind], axis, pairs + [(j, i) for i, j in pairs])  2.4 us
    select_n x2, other arithmetic, swapped(): strips = (jnp.where(even, high, low), jnp.where(even, low, high))  1.28 us
    slice x2, local copies, waits for them, and re-layouts, local(): broad = lambda s: jnp.concatenate([left[s], leaf_up[s], right[s]], axis=1)  1 us
  transfers between devices with their start and end apart: 4, of which 1 were waited for; matrix products, arithmetic and copies ran while one was open for 3% of the time, Pallas kernels for 16%

commit v1 on v0

--- a/solution.py
+++ b/solution.py
@@ -144,8 +144,10 @@
 @functools.lru_cache(maxsize=None)
 def plan():
     products = []
+    offsets = offset_table()
     for c, d in class_pairs():
-        for o, (dx, dy) in enumerate(offset_table()):
+        for o in sorted(range(len(offsets)), key=lambda o: (abs(offsets[o][1]) == 3, o)):
+            dx, dy = offsets[o]
             px, cs = divmod(c + dx, 2)
             py, ds = divmod(d + dy, 2)
             if abs(px) <= 1 and abs(py) <= 1:
@@ -369,19 +371,29 @@
 
     lax.fori_loop(0, 2, patch, 0)
 
+    shared = sum(abs(offset_table()[o][1]) < 3 for o, _ in plan()[:count])
+
+    def listed(i, s):
+        m = masks[i]
+        x = lut[entry_ref[i], s]
+        return jnp.concatenate([x[:, :128] * m, x[:, 128:] * m], axis=1)
+
     def interact(j, carry):
-        n, s = j // 2, j % 2
-        total = jnp.zeros((high, 256), F32)
-        for k in range(count):
+        n, s = 2 * (j // 2), j % 2
+        total = jnp.zeros((2 * high, 256), F32)
+        for k in range(shared):
             i = n * count + k
-            m = masks[i]
-            x = lut[entry_ref[i], s]
-            x = jnp.concatenate([x[:, :128] * m, x[:, 128:] * m], axis=1)
+            x = jnp.concatenate([listed(i, s), listed(i + count, s)], axis=0)
             total = total + dot(x, table[s, pick_ref[i]])
-        acc[s, n] = total
+        for d in range(2):
+            part = total[high * d : high * (d + 1)]
+            for k in range(shared, count):
+                i = (n + d) * count + k
+                part = part + dot(listed(i, s), table[s, pick_ref[i]])
+            acc[s, n + d] = part
         return carry
 
-    lax.fori_loop(0, 8, interact, 0)
+    lax.fori_loop(0, 4, interact, 0)
 
     check = None
     for s in range(2):
@@ -436,7 +448,7 @@
         in_specs=[VMEM] * 2,
         out_specs=VMEM,
         compiler_params=params(16),
-        cost_estimate=cost(rows * cols, 48, 16 * 1024 * 1024),
+        cost_estimate=cost(rows * cols, 48, 64 * 1024 * 1024),
     )(own, rotation)
 
 

time: 38 us -> 37 us (0.974)
  Pallas kernels: 18.8 us -> 17.9 us
    pallas_call x1, Pallas kernels: 12.8 us -> 11.9 us  [close_step(): pl.pallas_call(close_kernel, out_shape=jax.ShapeDtypeStruct(shape, F32),...]
where the time goes in v1:
time: 37 us; the launch traced here: 36.8 us
  Pallas kernels  17.9 us (48%)
  starting transfers between devices  8.85 us (24%)
  local copies, waits for them, and re-layouts  5.28 us (14%)
  waiting for transfers between devices  2.4 us (6%)
  other arithmetic  1.38 us (4%)
  between operations  0.96 us (3%)
    pallas_call x1, Pallas kernels, close_step(): pl.pallas_call(close_kernel, out_shape=jax.ShapeDtypeStruct(shape, F32),...  11.9 us
    ppermute x4, starting transfers between devices, swapped(): lax.ppermute(strips[kind], axis, pairs + [(j, i) for i, j in pairs])  8.85 us
    pallas_call x1, Pallas kernels, near_step(): pl.pallas_call(near_kernel, out_shape=(jax.ShapeDtypeStruct((pr, pc, dens...  5.44 us
    unnamed x32, local copies, waits for them, and re-layouts  4.28 us
    ppermute x4, waiting for transfers between devices, swapped(): lax.ppermute(strips[kind], axis, pairs + [(j, i) for i, j in pairs])  2.4 us
    select_n x2, other arithmetic, swapped(): strips = (jnp.where(even, high, low), jnp.where(even, low, high))  1.28 us
    slice x2, local copies, waits for them, and re-layouts, local(): broad = lambda s: jnp.concatenate([left[s], leaf_up[s], right[s]], axis=1)  1 us
  transfers between devices with their start and end apart: 4, of which 1 were waited for; matrix products, arithmetic and copies ran while one was open for 3% of the time, Pallas kernels for 16%

profile of v1, /device:TPU:12, one launch (start us, length us, event | category | flops | bytes accessed | tf_op | source)
XLA Modules:
  0.0 36.8 jit_solution(335460450758827383)
XLA Ops:
  0.6 1.2 %slice_select_fusion = (f32[24,4,456]{2,1,0:T(4,128)S(1)}, f32[24,4,456]{2,1,0:T(4,128)S(1)}) fusion(f32[24,16,456]{2,1,0:T(8,128)} %own_ref.3, pred[]{:T(512)} %eq.14), kind=kLoop, calls=%fused_computation.2 | loop fusion | flops 87552 | bytes 700417 | tf_op jit(solution)/shard_map/jit(_where)/select_n | solution.py:512
  1.8 0.1 collective-permute-start
  1.9 3.4 %collective-permute-start.1 = (f32[24,4,456]{2,1,0:T(4,128)S(1)}, f32[24,4,456]{2,1,0:T(4,128)S(1)}, u32[]{:S(2)}, u32[]{:S(2)}) collective-permute-start(f32[24,4,456]{2,1,0:T(4,128)S(1)} %get-tuple-element.22), channel_id=1, source_target_pairs={{1,2},{3,4},{5,6},{2,1},{4,3},{6,5},{9,10},{11,12},{13,14},{10,9},... | collective-permute-start | bytes 525320 | tf_op jit(solution)/shard_map/ppermute | solution.py:516
  5.4 1.0 %fusion.2 = (f32[4,16,456]{2,1,0:T(8,128)S(1)}, f32[4,16,456]{2,1,0:T(8,128)S(1)}) fusion(f32[24,16,456]{2,1,0:T(8,128)} %own_ref.3), kind=kLoop, calls=%fused_computation.9 | loop fusion | bytes 466944 | tf_op jit(solution)/shard_map/slice | solution.py:529
  6.4 0.1 add_convert_fusion.even_ref
  6.5 0.0 copy-start.2
  6.5 1.1 %copy-done.2 = f32[24,16,456]{2,1,0:T(8,128)S(1)} copy-done((f32[24,16,456]{2,1,0:T(8,128)S(1)}, f32[24,16,456]{2,1,0:T(8,128)}, u32[]{:S(2)}) %copy-start.2) | copy-done | bytes 700440
  7.6 0.0 copy-start.5
  7.6 1.0 %copy-done.5 = bf16[456,512]{1,0:T(8,128)(2,1)S(1)} copy-done((bf16[456,512]{1,0:T(8,128)(2,1)S(1)}, bf16[456,512]{1,0:T(8,128)(2,1)}, u32[]{:S(2)}) %copy-start.5) | copy-done | bytes 466968
  8.6 0.0 copy-start.3
  8.6 0.0 copy-start.6
  8.6 0.0 copy-start.11
  8.6 0.0 copy-start.12
  8.6 0.0 slice-start
  8.6 0.0 slice-start.1
  8.6 0.6 %shard_map.131.own_modes_ref = f32[4,24,16,128]{3,2,1,0:T(8,128)S(1)} custom-call(f32[24,16,456]{2,1,0:T(8,128)S(1)} %copy-done.2, bf16[456,512]{1,0:T(8,128)(2,1)S(1)} %copy-done.5), custom_call_target="tpu_custom_call" | custom-call | flops 2415919104 | bytes 67108864 | tf_op jit(solution)/shard_map/pallas_call | solution.py:445
  9.2 0.0 collective-permute-done.strip0_ref
  9.2 2.4 %collective-permute-done.1.strip1_ref = f32[24,4,456]{2,1,0:T(4,128)S(1)} collective-permute-done((f32[24,4,456]{2,1,0:T(4,128)S(1)}, f32[24,4,456]{2,1,0:T(4,128)S(1)}, u32[]{:S(2)}, u32[]{:S(2)}) %collective-permute-start.1) | collective-permute-done | bytes 175136 | tf_op jit(solution)/shard_map/ppermute | solution.py:516
  11.7 0.1 fusion
  11.8 0.1 collective-permute-start.2
  11.8 0.0 slice-start.2
  11.9 0.0 copy-start
  11.9 0.0 copy-start.1
  11.9 0.0 copy-start.4
  11.9 0.0 copy-start.7
  11.9 0.0 copy-start.8
  11.9 0.0 copy-start.9
  11.9 5.3 %collective-permute-start.3 = (f32[4,24,456]{2,1,0:T(8,128)S(1)}, f32[4,24,456]{2,1,0:T(8,128)S(1)}, u32[]{:S(2)}, u32[]{:S(2)}) collective-permute-start(f32[4,24,456]{2,1,0:T(8,128)S(1)} %get-tuple-element.24), channel_id=1, source_target_pairs={{8,16},{16,8},{9,17},{17,9},{10,18},{18,10},{11,19},{19,11},{12,20... | collective-permute-start | bytes 525320 | tf_op jit(solution)/shard_map/ppermute | solution.py:516
  17.2 0.0 copy-done.3
  17.2 0.0 copy-done.6
  17.2 0.0 copy-done.11
  17.2 0.0 copy-done.12
  17.3 0.0 copy-start.10
  17.3 2.0 %copy-done.10 = f32[4,456,456]{2,1,0:T(8,128)S(1)} copy-done((f32[4,456,456]{2,1,0:T(8,128)S(1)}, f32[4,456,456]{2,1,0:T(8,128)}, u32[]{:S(2)}) %copy-start.10) | copy-done | bytes 3327000
  19.3 5.4 %shard_map.132 = (f32[12,8,456]{2,1,0:T(8,128)}, bf16[36,2,128,256]{3,2,1,0:T(8,128)(2,1)S(1)}, f32[4,4,32,128]{3,2,1,0:T(8,128)S(1)}, f32[4,16,16,128]{3,2,1,0:...) custom-call(s32[2]{0:T(128)S(1)} %add_convert_fusion.even_ref, ...), custom_call_target="tpu_custom_call" | custom-call | flops 2415919104 | bytes 3326976 | tf_op jit(solution)/shard_map/pallas_call | solution.py:459
  24.8 0.0 collective-permute-done.2.end0_ref
  24.8 0.0 collective-permute-done.3.end1_ref
  24.8 0.0 slice-done
  24.8 0.0 slice-done.1
  24.8 0.0 slice-done.2
  24.8 0.0 copy-done
  24.8 0.0 copy-done.1
  24.8 0.0 copy-done.4
  24.8 0.0 copy-done.7
  24.8 0.0 copy-done.8
  24.9 0.0 copy-done.9
  24.9 11.9 %shard_map.133 = f32[24,16,456]{2,1,0:T(8,128)} custom-call(s32[108]{0:T(128)S(1)} %copy-done.8, s32[108]{0:T(128)S(1)} %copy-done.9, s32[2]{0:T(128)S(1)} %add_convert_fusion.even_ref, f32[4,24,456]{2,1,0:T(8,128)S(1)} %collective-permute-done.2.end0_ref, f32[4,24,456]{2,1,0:T(8,128)S(1)} %collective-permute-done.3.end1_ref, ...), custom_call_target="tpu_custom_call" | custom-call | flops 7549747200 | bytes 10485760 | tf_op jit(solution)/shard_map/pallas_call | solution.py:486
  (3 shorter events, 0.0 us)
Async XLA Ops:
  1.8 7.4 %collective-permute-start = (f32[24,4,456]{2,1,0:T(4,128)S(1)}, f32[24,4,456]{2,1,0:T(4,128)S(1)}, u32[]{:S(2)}, u32[]{:S(2)}) collective-permute-start(f32[24,4,456]{2,1,0:T(4,128)S(1)} %get-tuple-element.23), channel_id=1, source_target_pairs={{0,1},{2,3},{4,5},{6,7},{1,0},{3,2},{5,4},{7,6},{8,9},{10,11},{12,... | collective-permute-start | bytes 525320 | tf_op jit(solution)/shard_map/ppermute | solution.py:516
  1.9 9.7 %collective-permute-start.1 = (f32[24,4,456]{2,1,0:T(4,128)S(1)}, f32[24,4,456]{2,1,0:T(4,128)S(1)}, u32[]{:S(2)}, u32[]{:S(2)}) collective-permute-start(f32[24,4,456]{2,1,0:T(4,128)S(1)} %get-tuple-element.22), channel_id=1, source_target_pairs={{1,2},{3,4},{5,6},{2,1},{4,3},{6,5},{9,10},{11,12},{13,14},{10,9},... | collective-permute-start | bytes 525320 | tf_op jit(solution)/shard_map/ppermute | solution.py:516
  6.5 1.1 %copy-start.2 = (f32[24,16,456]{2,1,0:T(8,128)S(1)}, f32[24,16,456]{2,1,0:T(8,128)}, u32[]{:S(2)}) copy-start(f32[24,16,456]{2,1,0:T(8,128)} %own_ref.3) | copy-start | bytes 2101252
  7.6 1.0 %copy-start.5 = (bf16[456,512]{1,0:T(8,128)(2,1)S(1)}, bf16[456,512]{1,0:T(8,128)(2,1)}, u32[]{:S(2)}) copy-start(bf16[456,512]{1,0:T(8,128)(2,1)} %constant.40.clone.rot_ref) | copy-start | bytes 1400836
  8.6 8.6 %copy-start.3 = (f32[24,16,456]{2,1,0:T(8,128)S(1)}, f32[24,16,456]{2,1,0:T(8,128)}, u32[]{:S(2)}) copy-start(f32[24,16,456]{2,1,0:T(8,128)} %own_ref.3) | copy-start | bytes 2101252
  8.6 8.6 %copy-start.6 = (bf16[456,512]{1,0:T(8,128)(2,1)S(1)}, bf16[456,512]{1,0:T(8,128)(2,1)}, u32[]{:S(2)}) copy-start(bf16[456,512]{1,0:T(8,128)(2,1)} %constant.40.clone.rot_ref) | copy-start | bytes 1400836
  8.6 8.6 %copy-start.11 = (s32[24,16,40]{2,1,0:T(8,128)S(1)}, s32[24,16,40]{2,1,0:T(8,128)}, u32[]{:S(2)}) copy-start(s32[24,16,40]{2,1,0:T(8,128)} %llist_ref.1) | copy-start | bytes 184324
  8.6 8.6 %copy-start.12 = (s32[12,8,40]{2,1,0:T(8,128)S(1)}, s32[12,8,40]{2,1,0:T(8,128)}, u32[]{:S(2)}) copy-start(s32[12,8,40]{2,1,0:T(8,128)} %plist_ref.1) | copy-start | bytes 46084
  8.6 16.2 %slice-start = ((s8[10485760]{0:T(1024)(128)(4,1)}), s8[4194304]{0:T(1024)(128)(4,1)S(1)}, s32[]{:S(2)}) async-start(s8[10485760]{0:T(1024)(128)(4,1)} %bitcast.6), calls=%async_computation | async-start | bytes 8388608
  8.6 16.2 %slice-start.1 = ((s8[10485760]{0:T(1024)(128)(4,1)}), s8[4194304]{0:T(1024)(128)(4,1)S(1)}, s32[]{:S(2)}) async-start(s8[10485760]{0:T(1024)(128)(4,1)} %bitcast.6), calls=%async_computation.1 | async-start | bytes 8388608
  11.8 13.0 %collective-permute-start.2 = (f32[4,24,456]{2,1,0:T(8,128)S(1)}, f32[4,24,456]{2,1,0:T(8,128)S(1)}, u32[]{:S(2)}, u32[]{:S(2)}) collective-permute-start(f32[4,24,456]{2,1,0:T(8,128)S(1)} %get-tuple-element.25), channel_id=1, source_target_pairs={{0,8},{16,24},{8,0},{24,16},{1,9},{17,25},{9,1},{25,17},{2,10},{18... | collective-permute-start | bytes 525320 | tf_op jit(solution)/shard_map/ppermute | solution.py:516
  11.8 13.0 %slice-start.2 = ((s8[10485760]{0:T(1024)(128)(4,1)}), s8[2097152]{0:T(1024)(128)(4,1)S(1)}, s32[]{:S(2)}) async-start(s8[10485760]{0:T(1024)(128)(4,1)} %bitcast.6), calls=%async_computation.2 | async-start | bytes 4194304
  11.9 13.0 %copy-start = (f32[4,456,456]{2,1,0:T(8,128)S(1)}, f32[4,456,456]{2,1,0:T(8,128)}, u32[]{:S(2)}) copy-start(f32[4,456,456]{2,1,0:T(8,128)} %down_ref.1) | copy-start | bytes 9980932
  11.9 13.0 %copy-start.1 = (f32[456,456]{1,0:T(8,128)S(1)}, f32[456,456]{1,0:T(8,128)}, u32[]{:S(2)}) copy-start(f32[456,456]{1,0:T(8,128)} %inv_ref.1) | copy-start | bytes 2495236
  11.9 12.9 %copy-start.4 = (bf16[512,456]{1,0:T(8,128)(2,1)S(1)}, bf16[512,456]{1,0:T(8,128)(2,1)}, u32[]{:S(2)}) copy-start(bf16[512,456]{1,0:T(8,128)(2,1)} %constant.41.clone.back) | copy-start | bytes 1400836
  11.9 12.9 %copy-start.7 = (f32[12,8,456]{2,1,0:T(8,128)S(1)}, f32[12,8,456]{2,1,0:T(8,128)}, u32[]{:S(2)}) copy-start(f32[12,8,456]{2,1,0:T(8,128)} %pin_ref.1) | copy-start | bytes 525316
  11.9 12.9 %copy-start.8 = (s32[108]{0:T(128)S(1)}, s32[108]{0:T(128)}, u32[]{:S(2)}) copy-start(s32[108]{0:T(128)} %constant.43.clone.entry_ref) | copy-start | bytes 1300
  11.9 12.9 %copy-start.9 = (s32[108]{0:T(128)S(1)}, s32[108]{0:T(128)}, u32[]{:S(2)}) copy-start(s32[108]{0:T(128)} %constant.44.clone.pick_ref) | copy-start | bytes 1300
  11.9 12.8 %collective-permute-start.3 = (f32[4,24,456]{2,1,0:T(8,128)S(1)}, f32[4,24,456]{2,1,0:T(8,128)S(1)}, u32[]{:S(2)}, u32[]{:S(2)}) collective-permute-start(f32[4,24,456]{2,1,0:T(8,128)S(1)} %get-tuple-element.24), channel_id=1, source_target_pairs={{8,16},{16,8},{9,17},{17,9},{10,18},{18,10},{11,19},{19,11},{12,20... | collective-permute-start | bytes 525320 | tf_op jit(solution)/shard_map/ppermute | solution.py:516
  17.3 2.1 %copy-start.10 = (f32[4,456,456]{2,1,0:T(8,128)S(1)}, f32[4,456,456]{2,1,0:T(8,128)}, u32[]{:S(2)}) copy-start(f32[4,456,456]{2,1,0:T(8,128)} %up_ref.1) | copy-start | bytes 9980932

commit v2 on v1

--- a/solution.py
+++ b/solution.py
@@ -215,40 +215,38 @@
     )[:, :dens]
 
 
-def own_kernel(own_ref, rot_ref, modes_ref):
+def own_kernel(own_ref, rot_ref, modes_ref, tiled_ref, rot_out):
     rows, cols, dens = own_ref.shape
+    rot_out[...] = rot_ref[...]
     y = modes_of(own_ref[...].reshape(rows * cols, dens), rot_ref, dens)
-    for t in range(4):
+    for t, cut, to in cut_tiles(dens):
         modes_ref[t] = y[:, 128 * t : 128 * t + 128].reshape(rows, cols, 128)
-
-
-def near_kernel(
-    even_ref, strip0_ref, strip1_ref, own_ref, own_modes_ref, rot_ref, up_ref, llist_ref, plist_ref,
-    pup_ref, lut, edge_ref, pmodes_ref, masks_ref, upw_ref,
-    own_t, strip_t, modes, flat,
+        tiled_ref[t, :, :, to] = own_ref[:, :, cut]
+
+
+def pass_kernel(
+    even_ref, strip0_ref, strip1_ref, own_t, own_modes_ref, rot_ref, up_ref,
+    pup_ref, modes, pmodes, send0_ref, send1_ref,
+    strip_t,
 ):
-    rows, cols, dens = own_ref.shape
+    rows, _, dens = strip0_ref.shape
+    cols = own_modes_ref.shape[2]
     pr, pc = rows // 2, cols // 2
-    gr, gc = pr // 2, pc // 2
     boxes = pr * pc
-    used = boxes + gr * gc
-    high = lut.shape[2]
-    count = masks_ref.shape[0] // 4
-    even = even_ref[1] == 1
+    wide = cols + 2 * HALO
+    even_x, even_y = even_ref[0] == 1, even_ref[1] == 1
     for t, cut, to in cut_tiles(dens):
-        own_t[t, :, :, to] = own_ref[:, :, cut]
         first, second = strip0_ref[:, :, cut], strip1_ref[:, :, cut]
-        strip_t[t, :, 0:HALO, to] = jnp.where(even, second, first)
-        strip_t[t, :, HALO:, to] = jnp.where(even, first, second)
+        strip_t[t, :, 0:HALO, to] = jnp.where(even_y, second, first)
+        strip_t[t, :, HALO:, to] = jnp.where(even_y, first, second)
 
     parent = None
     for n, (c, d) in enumerate(class_pairs()):
-        upw_ref[n, 0], upw_ref[n, 1] = parts(up_ref[n])
         x = jnp.concatenate(
             [children(own_t, dens, (pr, pc), c, d), children(strip_t, dens, (pr, HALO), c, d)],
             axis=0,
         )
-        part = times_t(x, (upw_ref[n, 0], upw_ref[n, 1]))
+        part = times_t(x, parts(up_ref[n]))
         parent = part if parent is None else parent + part
     pup_ref[...] = parent[:boxes].reshape(pr, pc, dens)
     z = modes_of(jnp.concatenate([lanes(strip_t)[:, :dens], parent], axis=0), rot_ref, dens)
@@ -259,12 +257,25 @@
         strip = w[:, cut].reshape(rows, 8, 128)
         modes[t, 2 : 2 + rows, 4:8, :] = strip[:, 0:4]
         modes[t, 2 : 2 + rows, 8 + cols : 12 + cols, :] = strip[:, 4:8]
-        edge_ref[t, 0:2] = modes[t, 2:4]
-        edge_ref[t, 2:4] = modes[t, rows : rows + 2]
-        pmodes_ref[t, 2 : 2 + pr, 4 : 4 + pc, :] = p[:boxes, cut].reshape(pr, pc, 128)
+        pmodes[t, 2 : 2 + pr, 4 : 4 + pc, :] = p[:boxes, cut].reshape(pr, pc, 128)
         strip = p[boxes:, cut].reshape(pr, 4, 128)
-        pmodes_ref[t, 2 : 2 + pr, 2:4, :] = strip[:, 0:2]
-        pmodes_ref[t, 2 : 2 + pr, 4 + pc : 6 + pc, :] = strip[:, 2:4]
+        pmodes[t, 2 : 2 + pr, 2:4, :] = strip[:, 0:2]
+        pmodes[t, 2 : 2 + pr, 4 + pc : 6 + pc, :] = strip[:, 2:4]
+        low, high = modes[t, 2:4, 4 : 4 + wide, :], modes[t, rows : rows + 2, 4 : 4 + wide, :]
+        send0_ref[t, :, 0:wide, :] = jnp.where(even_x, high, low)
+        send1_ref[t, :, 0:wide, :] = jnp.where(even_x, low, high)
+        low, high = pmodes[t, 2:4, 2 : 6 + pc, :], pmodes[t, pr : pr + 2, 2 : 6 + pc, :]
+        send0_ref[t, :, wide : wide + 4 + pc, :] = jnp.where(even_x, high, low)
+        send1_ref[t, :, wide : wide + 4 + pc, :] = jnp.where(even_x, low, high)
+
+
+def near_kernel(modes, pmodes_ref, llist_ref, plist_ref, lut, masks_ref, flat):
+    rows, cols = modes.shape[1] - 4, modes.shape[2] - 16
+    pr, pc = rows // 2, cols // 2
+    gr, gc = pr // 2, pc // 2
+    used = pr * pc + gr * gc
+    high = lut.shape[2]
+    count = masks_ref.shape[0] // 4
 
     def gather(i, carry):
         base = 2 * (i % 3) + i // 3
@@ -305,44 +316,31 @@
 
 def close_kernel(
     entry_ref, pick_ref, even_ref,
-    end0_ref, end1_ref, edge_ref, pside_ref, upw_ref, masks, lut_ref,
-    rot_ref, pin_ref, back, table, down_ref, inv_ref,
+    got0_ref, got1_ref, modes, pside_ref, masks, lut_ref,
+    pin_ref, back, table, down_ref, inv_ref,
     out_ref,
-    ends_t, edge, pmodes, lut, acc, flat, plocal, sem,
+    edge, pmodes, lut, acc, flat, plocal, sem,
 ):
     rows, cols, dens = out_ref.shape
     pr, pc = rows // 2, cols // 2
     gr, gc = pr // 2, pc // 2
     boxes, pboxes = pr * pc, gr * gc
     high = lut.shape[2]
-    wide = end0_ref.shape[1]
+    wide = cols + 2 * HALO
     count = masks.shape[0] // 4
     copy = pltpu.make_async_copy(lut_ref, lut, sem)
     copy.start()
     even = even_ref[0] == 1
-    for t, cut, to in cut_tiles(dens):
-        first, second = end0_ref[:, :, cut], end1_ref[:, :, cut]
-        ends_t[t, 0:HALO, :, to] = jnp.where(even, second, first)
-        ends_t[t, HALO:, :, to] = jnp.where(even, first, second)
-    parent = None
-    for n, (c, d) in enumerate(class_pairs()):
-        x = children(ends_t, dens, (HALO, wide // 2), c, d)
-        part = times_t(x, (upw_ref[n, 0], upw_ref[n, 1]))
-        parent = part if parent is None else parent + part
-    x = lanes(ends_t, slice(HALO - 2, HALO + 2))[:, :dens]
-    y = modes_of(jnp.concatenate([x, parent], axis=0), rot_ref, dens)
-    z, p = y[: 4 * wide], y[4 * wide :]
     for t in range(4):
-        cut = slice(128 * t, 128 * t + 128)
-        end = z[:, cut].reshape(4, wide, 128)
-        edge[t, 0:2, 4 : 4 + wide, :] = end[0:2]
-        edge[t, 2:4] = edge_ref[t, 0:2]
-        edge[t, 4:6] = edge_ref[t, 2:4]
-        edge[t, 6:8, 4 : 4 + wide, :] = end[2:4]
-        end = p[:, cut].reshape(4, wide // 2, 128)
-        pmodes[t, 0:2, 2 : 2 + wide // 2, :] = end[0:2]
+        before = jnp.where(even, got1_ref[t], got0_ref[t])
+        after = jnp.where(even, got0_ref[t], got1_ref[t])
+        edge[t, 0:2, 4 : 4 + wide, :] = before[:, 0:wide]
+        edge[t, 2:4] = modes[t, 2:4]
+        edge[t, 4:6] = modes[t, rows : rows + 2]
+        edge[t, 6:8, 4 : 4 + wide, :] = after[:, 0:wide]
+        pmodes[t, 0:2, 2 : 6 + pc, :] = before[:, wide : wide + 4 + pc]
         pmodes[t, 2 : 2 + pr] = pside_ref[t, 2 : 2 + pr]
-        pmodes[t, 2 + pr :, 2 : 2 + wide // 2, :] = end[2:4]
+        pmodes[t, 2 + pr :, 2 : 6 + pc, :] = after[:, wide : wide + 4 + pc]
 
     copy.wait()
 
@@ -442,54 +440,66 @@
 
 def own_step(own, rotation):
     rows, cols, _ = own.shape
+    tiled = jax.ShapeDtypeStruct((4, rows, cols, 128), F32)
     return pl.pallas_call(
         own_kernel,
-        out_shape=jax.ShapeDtypeStruct((4, rows, cols, 128), F32),
+        out_shape=(tiled, tiled, jax.ShapeDtypeStruct(rotation.shape, BF16)),
         in_specs=[VMEM] * 2,
-        out_specs=VMEM,
+        out_specs=(VMEM,) * 3,
         compiler_params=params(16),
         cost_estimate=cost(rows * cols, 48, 64 * 1024 * 1024),
     )(own, rotation)
 
 
-def near_step(even, strips, own, own_modes, rotation, up, llist, plist):
-    rows, cols, dens = own.shape
+def pass_step(even, strips, tiled, own_modes, rotation, up):
+    rows, cols = tiled.shape[1:3]
+    dens = up.shape[1]
     pr, pc = rows // 2, cols // 2
-    high = height(pr * pc)
+    send = jax.ShapeDtypeStruct((4, 2, cols + 2 * HALO + 8 * ((pc + 11) // 8), 128), F32)
+    return pl.pallas_call(
+        pass_kernel,
+        out_shape=(
+            jax.ShapeDtypeStruct((pr, pc, dens), F32),
+            jax.ShapeDtypeStruct((4, rows + 4, cols + 16, 128), F32),
+            jax.ShapeDtypeStruct((4, pr + 4, pc + 8, 128), F32),
+            send,
+            send,
+        ),
+        in_specs=[SMEM] + [VMEM] * 6,
+        out_specs=(VMEM,) * 5,
+        scratch_shapes=[pltpu.VMEM((4, rows, 2 * HALO, 128), F32)],
+        compiler_params=params(16),
+        cost_estimate=cost(rows * cols, 32, up.size * 4),
+    )(even, *strips, tiled, own_modes, rotation, up)
+
+
+def near_step(modes, pmodes, llist, plist):
+    rows, cols, _ = llist.shape
+    high = height(rows * cols // 4)
     return pl.pallas_call(
         near_kernel,
         out_shape=(
-            jax.ShapeDtypeStruct((pr, pc, dens), F32),
             jax.ShapeDtypeStruct((36, 2, high, 256), BF16),
-            jax.ShapeDtypeStruct((4, 4, cols + 16, 128), F32),
-            jax.ShapeDtypeStruct((4, pr + 4, pc + 8, 128), F32),
             jax.ShapeDtypeStruct((len(plan()), high, 128), BF16),
-            jax.ShapeDtypeStruct((4, 2, dens, dens), BF16),
         ),
-        in_specs=[SMEM] + [VMEM] * 8,
-        out_specs=(VMEM,) * 6,
-        scratch_shapes=[
-            pltpu.VMEM((4, rows, cols, 128), F32),
-            pltpu.VMEM((4, rows, 2 * HALO, 128), F32),
-            pltpu.VMEM((4, rows + 4, cols + 16, 128), F32),
-            pltpu.VMEM((2, rows, cols, 128), F32),
-        ],
-        compiler_params=params(24),
-        cost_estimate=cost(rows * cols, 48, up.size * 4),
-    )(even, *strips, own, own_modes, rotation, up, llist, plist)
-
-
-def close_step(even, ends, edge, pmodes, upw, masks, lut, rotation, pin, back, table, down, inv, shape):
+        in_specs=[VMEM] * 4,
+        out_specs=(VMEM,) * 2,
+        scratch_shapes=[pltpu.VMEM((2, rows, cols, 128), F32)],
+        compiler_params=params(16),
+        cost_estimate=cost(rows * cols, 48, 16 * 1024 * 1024),
+    )(modes, pmodes, llist, plist)
+
+
+def close_step(even, ends, modes, pmodes, masks, lut, pin, back, table, down, inv, shape):
     rows, cols, dens = shape
     pr, pc = rows // 2, cols // 2
     high = height(pr * pc)
     return pl.pallas_call(
         close_kernel,
         out_shape=jax.ShapeDtypeStruct(shape, F32),
-        in_specs=[SMEM] * 3 + [VMEM] * 13,
+        in_specs=[SMEM] * 3 + [VMEM] * 11,
         out_specs=VMEM,
         scratch_shapes=[
-            pltpu.VMEM((4, 2 * HALO, cols + 2 * HALO, 128), F32),
             pltpu.VMEM((4, 8, cols + 16, 128), F32),
             pltpu.VMEM((4, pr + 4, pc + 8, 128), F32),
             pltpu.VMEM(lut.shape, BF16),
@@ -502,14 +512,12 @@
         cost_estimate=cost(rows * cols, 150, table.size * 2),
     )(
         jnp.asarray([e for _, e in plan()], jnp.int32), jnp.asarray([o for o, _ in plan()], jnp.int32),
-        even, *ends, edge, pmodes, upw, masks, lut, rotation, pin, back, table, down, inv,
+        even, *ends, modes, pmodes, masks, lut, pin, back, table, down, inv,
     )
 
 
-def swapped(low, high, axis, odd_first):
+def swapped(strips, axis, odd_first):
     peers = lax.axis_size(axis)
-    even = lax.axis_index(axis) % 2 == 0
-    strips = (jnp.where(even, high, low), jnp.where(even, low, high))
     got = [None, None]
     for kind in (1, 0) if odd_first else (0, 1):
         pairs = [(i, i + 1) for i in range(kind, peers - 1, 2)]
@@ -518,21 +526,19 @@
 
 
 def local(leaf_up, parent_in, leaf_lists, parent_lists, up_transfer, down_transfer, check_inverse):
-    rows, cols, _ = leaf_up.shape
+    cols = leaf_up.shape[1]
     even = [lax.axis_index(axis) % 2 == 0 for axis in ("gx", "gy")]
     flag = jnp.stack(even).astype(jnp.int32)
     rotation, back, table = (jnp.asarray(x) for x in operators())
-    strips = swapped(leaf_up[:, :HALO], leaf_up[:, cols - HALO :], "gy", True)
-    *strips, own_modes = lax.optimization_barrier((*strips, own_step(leaf_up, rotation)))
-    left = jnp.where(even[1], strips[1], strips[0])
-    right = jnp.where(even[1], strips[0], strips[1])
-    broad = lambda s: jnp.concatenate([left[s], leaf_up[s], right[s]], axis=1)
-    ends = swapped(broad(slice(0, HALO)), broad(slice(rows - HALO, rows)), "gx", False)
-    parent_up, lut, edge, pmodes, masks, upw = near_step(
-        flag, strips, leaf_up, own_modes, rotation, up_transfer, leaf_lists, parent_lists
-    )
+    low, high = leaf_up[:, :HALO], leaf_up[:, cols - HALO :]
+    strips = (jnp.where(even[1], high, low), jnp.where(even[1], low, high))
+    strips = swapped(strips, "gy", True)
+    own_modes, tiled, rotation = own_step(leaf_up, rotation)
+    parent_up, modes, pmodes, *sends = pass_step(flag, strips, tiled, own_modes, rotation, up_transfer)
+    ends = swapped(sends, "gx", False)
+    lut, masks = near_step(modes, pmodes, leaf_lists, parent_lists)
     leaf_down = close_step(
-        flag, ends, edge, pmodes, upw, masks, lut, rotation, parent_in, back, table,
+        flag, ends, modes, pmodes, masks, lut, parent_in, back, table,
         down_transfer, check_inverse, leaf_up.shape,
     )
     return leaf_down, parent_up

time: 37 us -> 33.3 us (0.90)
  the two profiles are of different devices: /device:TPU:12 before, /device:TPU:19 now
where the time goes in v2:
time: 33.3 us; the launch traced here: 33.1 us
  Pallas kernels  15.8 us (47%)
  starting transfers between devices  6.95 us (21%)
  waiting for transfers between devices  6.01 us (18%)
  local copies, waits for them, and re-layouts  2.21 us (7%)
  other arithmetic  1.27 us (4%)
  between operations  0.83 us (2%)
    pallas_call x1, Pallas kernels, close_step(): pl.pallas_call(close_kernel, out_shape=jax.ShapeDtypeStruct(shape, F32),...  9.93 us
    ppermute x4, starting transfers between devices, swapped(): lax.ppermute(strips[kind], axis, pairs + [(j, i) for i, j in pairs])  6.95 us
    ppermute x4, waiting for transfers between devices, swapped(): lax.ppermute(strips[kind], axis, pairs + [(j, i) for i, j in pairs])  6.01 us
    pallas_call x1, Pallas kernels, pass_step(): pl.pallas_call(pass_kernel, out_shape=(jax.ShapeDtypeStruct((pr, pc, dens...  2.73 us
    pallas_call x1, Pallas kernels, near_step(): pl.pallas_call(near_kernel, out_shape=(jax.ShapeDtypeStruct((36, 2, high,...  2.54 us
    unnamed x24, local copies, waits for them, and re-layouts  2.21 us
    select_n x1, other arithmetic, local(): strips = (jnp.where(even[1], high, low), jnp.where(even[1], low, high))  1.2 us
  transfers between devices with their start and end apart: 4, of which 2 were waited for; matrix products, arithmetic and copies ran while one was open for 0% of the time, Pallas kernels for 9%

profile of v2, /device:TPU:19, one launch (start us, length us, event | category | flops | bytes accessed | tf_op | source)
XLA Modules:
  0.0 33.1 jit_solution(10623501071494998263)
XLA Ops:
  0.6 1.2 %slice_select_fusion = (f32[24,4,456]{2,1,0:T(4,128)S(1)}, f32[24,4,456]{2,1,0:T(4,128)S(1)}) fusion(f32[24,16,456]{2,1,0:T(8,128)} %own_ref.1, pred[]{:T(512)} %eq.10), kind=kLoop, calls=%fused_computation | loop fusion | flops 87552 | bytes 700417 | tf_op jit(solution)/shard_map/jit(_where)/select_n | solution.py:534
  1.8 3.7 %collective-permute-start.1 = (f32[24,4,456]{2,1,0:T(4,128)S(1)}, f32[24,4,456]{2,1,0:T(4,128)S(1)}, u32[]{:S(2)}, u32[]{:S(2)}) collective-permute-start(f32[24,4,456]{2,1,0:T(4,128)S(1)} %get-tuple-element.22), channel_id=1, source_target_pairs={{1,2},{3,4},{5,6},{2,1},{4,3},{6,5},{9,10},{11,12},{13,14},{10,9},... | collective-permute-start | bytes 525320 | tf_op jit(solution)/shard_map/ppermute | solution.py:524
  5.5 0.1 collective-permute-start
  5.6 0.1 add_convert_fusion.even_ref
  5.7 0.0 copy-start.1
  5.7 1.1 %copy-done.1 = f32[24,16,456]{2,1,0:T(8,128)S(1)} copy-done((f32[24,16,456]{2,1,0:T(8,128)S(1)}, f32[24,16,456]{2,1,0:T(8,128)}, u32[]{:S(2)}) %copy-start.1) | copy-done | bytes 700440
  6.8 0.0 copy-start.9
  6.8 1.0 %copy-done.9 = bf16[456,512]{1,0:T(8,128)(2,1)S(1)} copy-done((bf16[456,512]{1,0:T(8,128)(2,1)S(1)}, bf16[456,512]{1,0:T(8,128)(2,1)}, u32[]{:S(2)}) %copy-start.9) | copy-done | bytes 466968
  7.9 0.0 copy-start
  7.9 0.0 copy-start.7
  7.9 0.6 %shard_map.131 = (f32[4,24,16,128]{3,2,1,0:T(8,128)S(1)}, f32[4,24,16,128]{3,2,1,0:T(8,128)S(1)}, bf16[456,512]{1,0:T(8,128)(2,1)S(1)}) custom-call(f32[24,16,456]{2,1,0:T(8,128)S(1)} %copy-done.1, bf16[456,512]{1,0:T(8,128)(2,1)S(1)} %copy-done.9), custom_call_target="tpu_custom_call" | custom-call | flops 2415919104 | bytes 67108864 | tf_op jit(solution)/shard_map/pallas_call | solution.py:444
  8.5 0.0 copy-start.4
  8.5 0.0 copy-start.6
  8.5 3.3 %collective-permute-done.1.strip1_ref = f32[24,4,456]{2,1,0:T(4,128)S(1)} collective-permute-done((f32[24,4,456]{2,1,0:T(4,128)S(1)}, f32[24,4,456]{2,1,0:T(4,128)S(1)}, u32[]{:S(2)}, u32[]{:S(2)}) %collective-permute-start.1) | collective-permute-done | bytes 175136 | tf_op jit(solution)/shard_map/ppermute | solution.py:524
  11.8 0.0 collective-permute-done.strip0_ref
  11.8 0.0 copy-done
  11.8 2.7 %shard_map.132 = (f32[12,8,456]{2,1,0:T(8,128)}, f32[4,28,32,128]{3,2,1,0:T(8,128)S(1)}, f32[4,16,16,128]{3,2,1,0:T(8,128)S(1)}, f32[4,2,40,128]{3,2,1,0:T(8,128)S(1)}, f32[4,2,40,128]{3,2,1,0:T(8,128)S(1)}) custom-call(s32[2]{0:T(128)S(1)} %add_convert_fusion.even_ref, f32[24,4,456]{2,1,0:T(4,128)S(1)} %collective-permute-done.strip0_ref, ...), custom_call_target="tpu_custom_call" | custom-call | flops 1610612736 | bytes 3326976 | tf_op jit(solution)/shard_map/pallas_call | solution.py:459
  14.5 1.3 %collective-permute-start.2 = (f32[4,2,40,128]{3,2,1,0:T(8,128)S(1)}, f32[4,2,40,128]{3,2,1,0:T(8,128)S(1)}, u32[]{:S(2)}, u32[]{:S(2)}) collective-permute-start(f32[4,2,40,128]{3,2,1,0:T(8,128)S(1)} %get-tuple-element.15), channel_id=1, source_target_pairs={{0,8},{16,24},{8,0},{24,16},{1,9},{17,25},{9,1},{25,17},{2,10},{18... | collective-permute-start | bytes 491528 | tf_op jit(solution)/shard_map/ppermute | solution.py:524
  15.8 1.9 %collective-permute-start.3 = (f32[4,2,40,128]{3,2,1,0:T(8,128)S(1)}, f32[4,2,40,128]{3,2,1,0:T(8,128)S(1)}, u32[]{:S(2)}, u32[]{:S(2)}) collective-permute-start(f32[4,2,40,128]{3,2,1,0:T(8,128)S(1)} %get-tuple-element.16), channel_id=1, source_target_pairs={{8,16},{16,8},{9,17},{17,9},{10,18},{18,10},{11,19},{19,11},{12,20... | collective-permute-start | bytes 491528 | tf_op jit(solution)/shard_map/ppermute | solution.py:524
  17.7 0.0 copy-done.4
  17.7 0.0 copy-done.6
  17.8 0.0 copy-start.2
  17.8 0.0 copy-start.3
  17.8 0.0 copy-start.5
  17.8 0.0 copy-start.8
  17.8 0.0 copy-start.10
  17.8 0.0 copy-start.11
  17.8 2.5 %shard_map.133 = (bf16[36,2,128,256]{3,2,1,0:T(8,128)(2,1)S(1)}, bf16[108,128,128]{2,1,0:T(8,128)(2,1)S(1)}) custom-call(f32[4,28,32,128]{3,2,1,0:T(8,128)S(1)} %get-tuple-element.17.modes, f32[4,16,16,128]{3,2,1,0:T(8,128)S(1)} %get-tuple-element.18.pmodes_ref.pside_ref, s32[24,16,40]{2,1,0:T(8,128)S(1)} %copy-done.4, s32[12,8,40]{2,1,0:T(8,128)S(1)} %copy-done.6), custom_call_target="tpu_custom_call" | custom-call | flops 2415919104 | bytes 16777216 | tf_op jit(solution)/shard_map/pallas_call | solution.py:479
  20.4 0.0 collective-permute-done.2.got0_ref
  20.4 2.7 %collective-permute-done.3.got1_ref = f32[4,2,40,128]{3,2,1,0:T(8,128)S(1)} collective-permute-done((f32[4,2,40,128]{3,2,1,0:T(8,128)S(1)}, f32[4,2,40,128]{3,2,1,0:T(8,128)S(1)}, u32[]{:S(2)}, u32[]{:S(2)}) %collective-permute-start.3) | collective-permute-done | bytes 163872 | tf_op jit(solution)/shard_map/ppermute | solution.py:524
  23.1 0.0 copy-done.7
  23.1 0.0 copy-done.2
  23.1 0.0 copy-done.3
  23.1 0.0 copy-done.5
  23.1 0.0 copy-done.8
  23.1 0.0 copy-done.10
  23.1 0.0 copy-done.11
  23.1 9.9 %shard_map.134 = f32[24,16,456]{2,1,0:T(8,128)} custom-call(s32[108]{0:T(128)S(1)} %copy-done.11, s32[108]{0:T(128)S(1)} %copy-done.10, s32[2]{0:T(128)S(1)} %add_convert_fusion.even_ref, f32[4,2,40,128]{3,2,1,0:T(8,128)S(1)} %collective-permute-done.2.got0_ref, f32[4,2,40,128]{3,2,1,0:T(8,128)S(1)} %collective-permute-done.3.got1_ref, ...), custom_call_target="tpu_custom_call" | custom-call | flops 7549747200 | bytes 10485760 | tf_op jit(solution)/shard_map/pallas_call | solution.py:497
Async XLA Ops:
  1.8 10.0 %collective-permute-start.1 = (f32[24,4,456]{2,1,0:T(4,128)S(1)}, f32[24,4,456]{2,1,0:T(4,128)S(1)}, u32[]{:S(2)}, u32[]{:S(2)}) collective-permute-start(f32[24,4,456]{2,1,0:T(4,128)S(1)} %get-tuple-element.22), channel_id=1, source_target_pairs={{1,2},{3,4},{5,6},{2,1},{4,3},{6,5},{9,10},{11,12},{13,14},{10,9},... | collective-permute-start | bytes 525320 | tf_op jit(solution)/shard_map/ppermute | solution.py:524
  5.5 6.3 %collective-permute-start = (f32[24,4,456]{2,1,0:T(4,128)S(1)}, f32[24,4,456]{2,1,0:T(4,128)S(1)}, u32[]{:S(2)}, u32[]{:S(2)}) collective-permute-start(f32[24,4,456]{2,1,0:T(4,128)S(1)} %get-tuple-element.23), channel_id=1, source_target_pairs={{0,1},{2,3},{4,5},{6,7},{1,0},{3,2},{5,4},{7,6},{8,9},{10,11},{12,... | collective-permute-start | bytes 525320 | tf_op jit(solution)/shard_map/ppermute | solution.py:524
  5.7 1.1 %copy-start.1 = (f32[24,16,456]{2,1,0:T(8,128)S(1)}, f32[24,16,456]{2,1,0:T(8,128)}, u32[]{:S(2)}) copy-start(f32[24,16,456]{2,1,0:T(8,128)} %own_ref.1) | copy-start | bytes 2101252
  6.8 1.0 %copy-start.9 = (bf16[456,512]{1,0:T(8,128)(2,1)S(1)}, bf16[456,512]{1,0:T(8,128)(2,1)}, u32[]{:S(2)}) copy-start(bf16[456,512]{1,0:T(8,128)(2,1)} %constant.36.clone.rot_ref) | copy-start | bytes 1400836
  7.9 3.9 %copy-start = (f32[4,456,456]{2,1,0:T(8,128)S(1)}, f32[4,456,456]{2,1,0:T(8,128)}, u32[]{:S(2)}) copy-start(f32[4,456,456]{2,1,0:T(8,128)} %up_ref.1) | copy-start | bytes 9980932
  7.9 15.2 %copy-start.7 = (bf16[2,40,256,256]{3,2,1,0:T(8,128)(2,1)S(1)}, bf16[2,40,256,256]{3,2,1,0:T(8,128)(2,1)}, u32[]{:S(2)}) copy-start(bf16[2,40,256,256]{3,2,1,0:T(8,128)(2,1)} %constant.38.clone.table) | copy-start | bytes 31457284
  8.5 9.3 %copy-start.4 = (s32[24,16,40]{2,1,0:T(8,128)S(1)}, s32[24,16,40]{2,1,0:T(8,128)}, u32[]{:S(2)}) copy-start(s32[24,16,40]{2,1,0:T(8,128)} %llist_ref.1) | copy-start | bytes 184324
  8.5 9.3 %copy-start.6 = (s32[12,8,40]{2,1,0:T(8,128)S(1)}, s32[12,8,40]{2,1,0:T(8,128)}, u32[]{:S(2)}) copy-start(s32[12,8,40]{2,1,0:T(8,128)} %plist_ref.1) | copy-start | bytes 46084
  14.5 5.8 %collective-permute-start.2 = (f32[4,2,40,128]{3,2,1,0:T(8,128)S(1)}, f32[4,2,40,128]{3,2,1,0:T(8,128)S(1)}, u32[]{:S(2)}, u32[]{:S(2)}) collective-permute-start(f32[4,2,40,128]{3,2,1,0:T(8,128)S(1)} %get-tuple-element.15), channel_id=1, source_target_pairs={{0,8},{16,24},{8,0},{24,16},{1,9},{17,25},{9,1},{25,17},{2,10},{18... | collective-permute-start | bytes 491528 | tf_op jit(solution)/shard_map/ppermute | solution.py:524
  15.8 7.3 %collective-permute-start.3 = (f32[4,2,40,128]{3,2,1,0:T(8,128)S(1)}, f32[4,2,40,128]{3,2,1,0:T(8,128)S(1)}, u32[]{:S(2)}, u32[]{:S(2)}) collective-permute-start(f32[4,2,40,128]{3,2,1,0:T(8,128)S(1)} %get-tuple-element.16), channel_id=1, source_target_pairs={{8,16},{16,8},{9,17},{17,9},{10,18},{18,10},{11,19},{19,11},{12,20... | collective-permute-start | bytes 491528 | tf_op jit(solution)/shard_map/ppermute | solution.py:524
  17.8 5.3 %copy-start.2 = (f32[4,456,456]{2,1,0:T(8,128)S(1)}, f32[4,456,456]{2,1,0:T(8,128)}, u32[]{:S(2)}) copy-start(f32[4,456,456]{2,1,0:T(8,128)} %down_ref.1) | copy-start | bytes 9980932
  17.8 5.3 %copy-start.3 = (f32[456,456]{1,0:T(8,128)S(1)}, f32[456,456]{1,0:T(8,128)}, u32[]{:S(2)}) copy-start(f32[456,456]{1,0:T(8,128)} %inv_ref.1) | copy-start | bytes 2495236
  17.8 5.3 %copy-start.5 = (f32[12,8,456]{2,1,0:T(8,128)S(1)}, f32[12,8,456]{2,1,0:T(8,128)}, u32[]{:S(2)}) copy-start(f32[12,8,456]{2,1,0:T(8,128)} %pin_ref.1) | copy-start | bytes 525316
  17.8 5.3 %copy-start.8 = (bf16[512,456]{1,0:T(8,128)(2,1)S(1)}, bf16[512,456]{1,0:T(8,128)(2,1)}, u32[]{:S(2)}) copy-start(bf16[512,456]{1,0:T(8,128)(2,1)} %constant.37.clone.back) | copy-start | bytes 1400836
  17.8 5.3 %copy-start.10 = (s32[108]{0:T(128)S(1)}, s32[108]{0:T(128)}, u32[]{:S(2)}) copy-start(s32[108]{0:T(128)} %constant.40.clone.pick_ref) | copy-start | bytes 1300
  17.8 5.3 %copy-start.11 = (s32[108]{0:T(128)S(1)}, s32[108]{0:T(128)}, u32[]{:S(2)}) copy-start(s32[108]{0:T(128)} %constant.39.clone.entry_ref) | copy-start | bytes 1300

commit v3 on v2

--- a/solution.py
+++ b/solution.py
@@ -224,8 +224,16 @@
         tiled_ref[t, :, :, to] = own_ref[:, :, cut]
 
 
+def split_kernel(weight_ref, after_ref, split_ref):
+    def one(n, carry):
+        split_ref[n, 0], split_ref[n, 1] = parts(weight_ref[n])
+        return carry
+
+    lax.fori_loop(0, weight_ref.shape[0], one, 0)
+
+
 def pass_kernel(
-    even_ref, strip0_ref, strip1_ref, own_t, own_modes_ref, rot_ref, up_ref,
+    even_ref, strip0_ref, strip1_ref, own_t, own_modes_ref, rot_ref, upw_ref,
     pup_ref, modes, pmodes, send0_ref, send1_ref,
     strip_t,
 ):
@@ -246,7 +254,7 @@
             [children(own_t, dens, (pr, pc), c, d), children(strip_t, dens, (pr, HALO), c, d)],
             axis=0,
         )
-        part = times_t(x, parts(up_ref[n]))
+        part = times_t(x, (upw_ref[n, 0], upw_ref[n, 1]))
         parent = part if parent is None else parent + part
     pup_ref[...] = parent[:boxes].reshape(pr, pc, dens)
     z = modes_of(jnp.concatenate([lanes(strip_t)[:, :dens], parent], axis=0), rot_ref, dens)
@@ -269,7 +277,11 @@
         send1_ref[t, :, wide : wide + 4 + pc, :] = jnp.where(even_x, low, high)
 
 
-def near_kernel(modes, pmodes_ref, llist_ref, plist_ref, lut, masks_ref, flat):
+def near_kernel(
+    modes, pmodes_ref, llist_ref, plist_ref, down_ref, inv_ref,
+    lut, masks_ref, downw_ref, invw_ref,
+    flat,
+):
     rows, cols = modes.shape[1] - 4, modes.shape[2] - 16
     pr, pc = rows // 2, cols // 2
     gr, gc = pr // 2, pc // 2
@@ -300,6 +312,13 @@
 
     lax.fori_loop(0, 6, gather, 0)
 
+    def halve(n, carry):
+        downw_ref[n, 0], downw_ref[n, 1] = parts(down_ref[n])
+        return carry
+
+    lax.fori_loop(0, 4, halve, 0)
+    invw_ref[0], invw_ref[1] = parts(inv_ref[...])
+
     flat[0, :, :, 0 : llist_ref.shape[2]] = llist_ref[...].astype(F32)
     flat[1, 0:pr, 0:pc, 0 : plist_ref.shape[2]] = plist_ref[...].astype(F32)
     for n, (c, d) in enumerate(class_pairs()):
@@ -317,9 +336,9 @@
 def close_kernel(
     entry_ref, pick_ref, even_ref,
     got0_ref, got1_ref, modes, pside_ref, masks, lut_ref,
-    pin_ref, back, table, down_ref, inv_ref,
+    pin_ref, back, table, downw, invw,
     out_ref,
-    edge, pmodes, lut, acc, flat, plocal, sem,
+    edge, pmodes, lut, acc, flat, plocal, checks, sem,
 ):
     rows, cols, dens = out_ref.shape
     pr, pc = rows // 2, cols // 2
@@ -398,21 +417,22 @@
         part = times_exact(acc[s].reshape(4 * high, 256), back[256 * s : 256 * (s + 1)])
         check = part if check is None else check + part
 
-    inverse = parts(inv_ref[...])
+    inverse = (invw[0], invw[1])
     for n, (c, d) in enumerate(class_pairs()):
         for t, cut, to in cut_tiles(dens):
             for j in range(gr):
                 r = high * n + boxes + gc * j
                 plocal[t, 2 * j + c, pl.ds(d, gc, stride=2), to] = check[r : r + gc, cut]
     local = pin_ref[...].reshape(boxes, dens) + times_t(lanes(plocal)[:, :dens], inverse)
-    x = jnp.concatenate(
-        [
-            check[high * n : high * n + boxes] + times_t(local, parts(down_ref[n]))
-            for n in range(4)
-        ],
-        axis=0,
-    )
-    result = times_t(x, inverse)
+    checks[...] = jnp.concatenate([check[high * n : high * n + boxes] for n in range(4)], axis=0)
+
+    def spread(n, carry):
+        at = pl.ds(pl.multiple_of(boxes * n, 8), boxes)
+        checks[at, :] += times_t(local, (downw[n, 0], downw[n, 1]))
+        return carry
+
+    lax.fori_loop(0, 4, spread, 0)
+    result = times_t(checks[...], inverse)
     for n, (c, d) in enumerate(class_pairs()):
         for t, cut, to in cut_tiles(dens):
             for j in range(pr):
@@ -446,14 +466,26 @@
         out_shape=(tiled, tiled, jax.ShapeDtypeStruct(rotation.shape, BF16)),
         in_specs=[VMEM] * 2,
         out_specs=(VMEM,) * 3,
-        compiler_params=params(16),
+        compiler_params=params(12),
         cost_estimate=cost(rows * cols, 48, 64 * 1024 * 1024),
     )(own, rotation)
 
 
-def pass_step(even, strips, tiled, own_modes, rotation, up):
+def split_step(weight, after):
+    n, dens, _ = weight.shape
+    return pl.pallas_call(
+        split_kernel,
+        out_shape=jax.ShapeDtypeStruct((n, 2, dens, dens), BF16),
+        in_specs=[VMEM] * 2,
+        out_specs=VMEM,
+        compiler_params=params(12),
+        cost_estimate=cost(8 * dens, 1, weight.size * 8),
+    )(weight, after)
+
+
+def pass_step(even, strips, tiled, own_modes, rotation, upw):
     rows, cols = tiled.shape[1:3]
-    dens = up.shape[1]
+    dens = upw.shape[2]
     pr, pc = rows // 2, cols // 2
     send = jax.ShapeDtypeStruct((4, 2, cols + 2 * HALO + 8 * ((pc + 11) // 8), 128), F32)
     return pl.pallas_call(
@@ -468,12 +500,12 @@
         in_specs=[SMEM] + [VMEM] * 6,
         out_specs=(VMEM,) * 5,
         scratch_shapes=[pltpu.VMEM((4, rows, 2 * HALO, 128), F32)],
-        compiler_params=params(16),
-        cost_estimate=cost(rows * cols, 32, up.size * 4),
-    )(even, *strips, tiled, own_modes, rotation, up)
-
-
-def near_step(modes, pmodes, llist, plist):
+        compiler_params=params(12),
+        cost_estimate=cost(rows * cols, 32, upw.size * 2),
+    )(even, *strips, tiled, own_modes, rotation, upw)
+
+
+def near_step(modes, pmodes, llist, plist, down, inv):
     rows, cols, _ = llist.shape
     high = height(rows * cols // 4)
     return pl.pallas_call(
@@ -481,16 +513,18 @@
         out_shape=(
             jax.ShapeDtypeStruct((36, 2, high, 256), BF16),
             jax.ShapeDtypeStruct((len(plan()), high, 128), BF16),
+            jax.ShapeDtypeStruct((4, 2) + inv.shape, BF16),
+            jax.ShapeDtypeStruct((2,) + inv.shape, BF16),
         ),
-        in_specs=[VMEM] * 4,
-        out_specs=(VMEM,) * 2,
+        in_specs=[VMEM] * 6,
+        out_specs=(VMEM,) * 4,
         scratch_shapes=[pltpu.VMEM((2, rows, cols, 128), F32)],
-        compiler_params=params(16),
+        compiler_params=params(12),
         cost_estimate=cost(rows * cols, 48, 16 * 1024 * 1024),
-    )(modes, pmodes, llist, plist)
-
-
-def close_step(even, ends, modes, pmodes, masks, lut, pin, back, table, down, inv, shape):
+    )(modes, pmodes, llist, plist, down, inv)
+
+
+def close_step(even, ends, modes, pmodes, masks, lut, pin, back, table, downw, invw, shape):
     rows, cols, dens = shape
     pr, pc = rows // 2, cols // 2
     high = height(pr * pc)
@@ -506,13 +540,14 @@
             pltpu.VMEM((2, 4, high, 256), F32),
             pltpu.VMEM((4, rows, cols, 128), F32),
             pltpu.VMEM((4, pr, pc, 128), F32),
+            pltpu.VMEM((4 * pr * pc, dens), F32),
             pltpu.SemaphoreType.DMA,
         ],
         compiler_params=params(24),
         cost_estimate=cost(rows * cols, 150, table.size * 2),
     )(
         jnp.asarray([e for _, e in plan()], jnp.int32), jnp.asarray([o for o, _ in plan()], jnp.int32),
-        even, *ends, modes, pmodes, masks, lut, pin, back, table, down, inv,
+        even, *ends, modes, pmodes, masks, lut, pin, back, table, downw, invw,
     )
 
 
@@ -534,12 +569,15 @@
     strips = (jnp.where(even[1], high, low), jnp.where(even[1], low, high))
     strips = swapped(strips, "gy", True)
     own_modes, tiled, rotation = own_step(leaf_up, rotation)
-    parent_up, modes, pmodes, *sends = pass_step(flag, strips, tiled, own_modes, rotation, up_transfer)
+    upw = split_step(up_transfer, rotation)
+    parent_up, modes, pmodes, *sends = pass_step(flag, strips, tiled, own_modes, rotation, upw)
     ends = swapped(sends, "gx", False)
-    lut, masks = near_step(modes, pmodes, leaf_lists, parent_lists)
+    lut, masks, downw, invw = near_step(
+        modes, pmodes, leaf_lists, parent_lists, down_transfer, check_inverse
+    )
     leaf_down = close_step(
         flag, ends, modes, pmodes, masks, lut, parent_in, back, table,
-        down_transfer, check_inverse, leaf_up.shape,
+        downw, invw, leaf_up.shape,
     )
     return leaf_down, parent_up
 

time: 33.3 us -> 38.3 us (1.15)
  local copies, waits for them, and re-layouts: 2.21 us -> 8.23 us
  waiting for transfers between devices: 6.01 us -> 3.06 us
  Pallas kernels: 15.8 us -> 17.5 us
    unnamed x24, local copies, waits for them, and re-layouts: 2.21 us -> 8.23 us
    ppermute x4, waiting for transfers between devices: 6.01 us -> 3.06 us  [swapped(): lax.ppermute(strips[kind], axis, pairs + [(j, i) for i, j in pairs])]
    pallas_call x1, Pallas kernels: 2.54 us -> 3.25 us  [near_step(): pl.pallas_call(near_kernel, out_shape=(jax.ShapeDtypeStruct((36, 2, high,...]
    pallas_call x0 -> x1, Pallas kernels: none -> 0.54 us  [split_step(): pl.pallas_call(split_kernel, out_shape=jax.ShapeDtypeStruct((n, 2, dens,...]
    pallas_call x1, Pallas kernels: 9.93 us -> 10.5 us  [close_step(): pl.pallas_call(close_kernel, out_shape=jax.ShapeDtypeStruct(shape, F32),...]
  transfers between devices with their start and end apart: 4 -> 4, of which waited for: 2 -> 2; matrix products, arithmetic and copies ran while one was open for 0% -> 0% of each run, Pallas kernels for 9% -> 12%
where the time goes in v3:
time: 38.3 us; the launch traced here: 37.8 us
  Pallas kernels  17.5 us (46%)
  local copies, waits for them, and re-layouts  8.23 us (21%)
  starting transfers between devices  6.95 us (18%)
  waiting for transfers between devices  3.06 us (8%)
  other arithmetic  1.28 us (3%)
  between operations  0.84 us (2%)
    pallas_call x1, Pallas kernels, close_step(): pl.pallas_call(close_kernel, out_shape=jax.ShapeDtypeStruct(shape, F32),...  10.5 us
    unnamed x24, local copies, waits for them, and re-layouts  8.23 us
    ppermute x4, starting transfers between devices, swapped(): lax.ppermute(strips[kind], axis, pairs + [(j, i) for i, j in pairs])  6.95 us
    pallas_call x1, Pallas kernels, near_step(): pl.pallas_call(near_kernel, out_shape=(jax.ShapeDtypeStruct((36, 2, high,...  3.25 us
    ppermute x4, waiting for transfers between devices, swapped(): lax.ppermute(strips[kind], axis, pairs + [(j, i) for i, j in pairs])  3.06 us
    pallas_call x1, Pallas kernels, pass_step(): pl.pallas_call(pass_kernel, out_shape=(jax.ShapeDtypeStruct((pr, pc, dens...  2.62 us
    select_n x1, other arithmetic, local(): strips = (jnp.where(even[1], high, low), jnp.where(even[1], low, high))  1.2 us
  transfers between devices with their start and end apart: 4, of which 2 were waited for; matrix products, arithmetic and copies ran while one was open for 0% of the time, Pallas kernels for 12%

profile of v3, /device:TPU:19, one launch (start us, length us, event | category | flops | bytes accessed | tf_op | source)
XLA Modules:
  0.0 37.8 jit_solution(11613278078073323715)
XLA Ops:
  0.6 1.2 %slice_select_fusion = (f32[24,4,456]{2,1,0:T(4,128)S(1)}, f32[24,4,456]{2,1,0:T(4,128)S(1)}) fusion(f32[24,16,456]{2,1,0:T(8,128)} %own_ref.1, pred[]{:T(512)} %eq.10), kind=kLoop, calls=%fused_computation | loop fusion | flops 87552 | bytes 700417 | tf_op jit(solution)/shard_map/jit(_where)/select_n | solution.py:569
  1.8 3.7 %collective-permute-start.1 = (f32[24,4,456]{2,1,0:T(4,128)S(1)}, f32[24,4,456]{2,1,0:T(4,128)S(1)}, u32[]{:S(2)}, u32[]{:S(2)}) collective-permute-start(f32[24,4,456]{2,1,0:T(4,128)S(1)} %get-tuple-element.26), channel_id=1, source_target_pairs={{1,2},{3,4},{5,6},{2,1},{4,3},{6,5},{9,10},{11,12},{13,14},{10,9},... | collective-permute-start | bytes 525320 | tf_op jit(solution)/shard_map/ppermute | solution.py:559
  5.5 0.1 collective-permute-start
  5.6 0.0 copy-start.1
  5.6 1.1 %copy-done.1 = f32[24,16,456]{2,1,0:T(8,128)S(1)} copy-done((f32[24,16,456]{2,1,0:T(8,128)S(1)}, f32[24,16,456]{2,1,0:T(8,128)}, u32[]{:S(2)}) %copy-start.1) | copy-done | bytes 700440
  6.7 0.0 copy-start.9
  6.7 1.0 %copy-done.9 = bf16[456,512]{1,0:T(8,128)(2,1)S(1)} copy-done((bf16[456,512]{1,0:T(8,128)(2,1)S(1)}, bf16[456,512]{1,0:T(8,128)(2,1)}, u32[]{:S(2)}) %copy-start.9) | copy-done | bytes 466968
  7.8 0.6 %shard_map.131 = (f32[4,24,16,128]{3,2,1,0:T(8,128)S(1)}, f32[4,24,16,128]{3,2,1,0:T(8,128)S(1)}, bf16[456,512]{1,0:T(8,128)(2,1)S(1)}) custom-call(f32[24,16,456]{2,1,0:T(8,128)S(1)} %copy-done.1, bf16[456,512]{1,0:T(8,128)(2,1)S(1)} %copy-done.9), custom_call_target="tpu_custom_call" | custom-call | flops 2415919104 | bytes 67108864 | tf_op jit(solution)/shard_map/pallas_call | solution.py:464
  8.4 0.0 copy-start
  8.4 2.0 %copy-done = f32[4,456,456]{2,1,0:T(8,128)S(1)} copy-done((f32[4,456,456]{2,1,0:T(8,128)S(1)}, f32[4,456,456]{2,1,0:T(8,128)}, u32[]{:S(2)}) %copy-start) | copy-done | bytes 3327000
  10.4 0.5 %shard_map.132.upw_ref = bf16[4,2,456,456]{3,2,1,0:T(8,128)(2,1)S(1)} custom-call(f32[4,456,456]{2,1,0:T(8,128)S(1)} %copy-done, bf16[456,512]{1,0:T(8,128)(2,1)S(1)} %get-tuple-element.16.after_ref.rot_ref), custom_call_target="tpu_custom_call" | custom-call | flops 478150656 | bytes 6653952 | tf_op jit(solution)/shard_map/pallas_call | solution.py:476
  11.0 0.0 copy-start.2
  11.0 0.0 copy-start.3
  11.0 0.0 copy-start.4
  11.0 0.0 copy-start.6
  11.0 0.1 add_convert_fusion.even_ref
  11.1 0.7 %collective-permute-done.1.strip1_ref = f32[24,4,456]{2,1,0:T(4,128)S(1)} collective-permute-done((f32[24,4,456]{2,1,0:T(4,128)S(1)}, f32[24,4,456]{2,1,0:T(4,128)S(1)}, u32[]{:S(2)}, u32[]{:S(2)}) %collective-permute-start.1) | collective-permute-done | bytes 175136 | tf_op jit(solution)/shard_map/ppermute | solution.py:559
  11.8 0.0 collective-permute-done.strip0_ref
  11.8 2.6 %shard_map.133 = (f32[12,8,456]{2,1,0:T(8,128)}, f32[4,28,32,128]{3,2,1,0:T(8,128)S(1)}, f32[4,16,16,128]{3,2,1,0:T(8,128)S(1)}, f32[4,2,40,128]{3,2,1,0:T(8,128)S(1)}, f32[4,2,40,128]{3,2,1,0:T(8,128)S(1)}) custom-call(s32[2]{0:T(128)S(1)} %add_convert_fusion.even_ref, f32[24,4,456]{2,1,0:T(4,128)S(1)} %collective-permute-done.strip0_ref, ...), custom_call_target="tpu_custom_call" | custom-call | flops 1610612736 | bytes 3326976 | tf_op jit(solution)/shard_map/pallas_call | solution.py:491
  14.4 1.3 %collective-permute-start.2 = (f32[4,2,40,128]{3,2,1,0:T(8,128)S(1)}, f32[4,2,40,128]{3,2,1,0:T(8,128)S(1)}, u32[]{:S(2)}, u32[]{:S(2)}) collective-permute-start(f32[4,2,40,128]{3,2,1,0:T(8,128)S(1)} %get-tuple-element.17), channel_id=1, source_target_pairs={{0,8},{16,24},{8,0},{24,16},{1,9},{17,25},{9,1},{25,17},{2,10},{18... | collective-permute-start | bytes 491528 | tf_op jit(solution)/shard_map/ppermute | solution.py:559
  15.7 1.9 %collective-permute-start.3 = (f32[4,2,40,128]{3,2,1,0:T(8,128)S(1)}, f32[4,2,40,128]{3,2,1,0:T(8,128)S(1)}, u32[]{:S(2)}, u32[]{:S(2)}) collective-permute-start(f32[4,2,40,128]{3,2,1,0:T(8,128)S(1)} %get-tuple-element.18), channel_id=1, source_target_pairs={{8,16},{16,8},{9,17},{17,9},{10,18},{18,10},{11,19},{19,11},{12,20... | collective-permute-start | bytes 491528 | tf_op jit(solution)/shard_map/ppermute | solution.py:559
  17.6 0.0 copy-done.2
  17.6 0.0 copy-done.3
  17.7 0.0 copy-done.4
  17.7 0.0 copy-done.6
  17.7 0.0 copy-start.5
  17.7 0.0 copy-start.8
  17.7 0.0 copy-start.10
  17.7 0.0 copy-start.11
  17.7 3.3 %shard_map.134 = (bf16[36,2,128,256]{3,2,1,0:T(8,128)(2,1)S(1)}, bf16[108,128,128]{2,1,0:T(8,128)(2,1)S(1)}, bf16[4,2,456,456]{3,2,1,0:T(8,128)(2,1)S(1)}, bf16[2,456,456]{2,1,0:T(8,128)(2,1)S(1)}) custom-call(f32[4,28,32,128]{3,2,1,0:T(8,128)S(1)} %get-tuple-element.19.modes, f32[4,16,16,128]{3,2,1,0:T(8,128)S(1)} %get-tuple-element.20.pmodes_ref.pside_ref, ...), custom_call_target="tpu_custom_call" | custom-call | flops 2415919104 | bytes 16777216 | tf_op jit(solution)/shard_map/pallas_call | solution.py:511
  21.0 0.0 collective-permute-done.2.got0_ref
  21.0 2.4 %collective-permute-done.3.got1_ref = f32[4,2,40,128]{3,2,1,0:T(8,128)S(1)} collective-permute-done((f32[4,2,40,128]{3,2,1,0:T(8,128)S(1)}, f32[4,2,40,128]{3,2,1,0:T(8,128)S(1)}, u32[]{:S(2)}, u32[]{:S(2)}) %collective-permute-start.3) | collective-permute-done | bytes 163872 | tf_op jit(solution)/shard_map/ppermute | solution.py:559
  23.4 0.0 copy-done.5
  23.4 0.0 copy-done.8
  23.4 0.0 copy-done.10
  23.4 0.0 copy-done.11
  23.4 0.0 copy-start.7
  23.4 4.0 %copy-done.7 = bf16[2,40,256,256]{3,2,1,0:T(8,128)(2,1)S(1)} copy-done((bf16[2,40,256,256]{3,2,1,0:T(8,128)(2,1)S(1)}, bf16[2,40,256,256]{3,2,1,0:T(8,128)(2,1)}, u32[]{:S(2)}) %copy-start.7) | copy-done | bytes 10485784
  27.4 10.5 %shard_map.135 = f32[24,16,456]{2,1,0:T(8,128)} custom-call(s32[108]{0:T(128)S(1)} %copy-done.11, s32[108]{0:T(128)S(1)} %copy-done.10, s32[2]{0:T(128)S(1)} %add_convert_fusion.even_ref, f32[4,2,40,128]{3,2,1,0:T(8,128)S(1)} %collective-permute-done.2.got0_ref, f32[4,2,40,128]{3,2,1,0:T(8,128)S(1)} %collective-permute-done.3.got1_ref, ...), custom_call_target="tpu_custom_call" | custom-call | flops 7549747200 | bytes 10485760 | tf_op jit(solution)/shard_map/pallas_call | solution.py:531
Async XLA Ops:
  1.8 10.0 %collective-permute-start.1 = (f32[24,4,456]{2,1,0:T(4,128)S(1)}, f32[24,4,456]{2,1,0:T(4,128)S(1)}, u32[]{:S(2)}, u32[]{:S(2)}) collective-permute-start(f32[24,4,456]{2,1,0:T(4,128)S(1)} %get-tuple-element.26), channel_id=1, source_target_pairs={{1,2},{3,4},{5,6},{2,1},{4,3},{6,5},{9,10},{11,12},{13,14},{10,9},... | collective-permute-start | bytes 525320 | tf_op jit(solution)/shard_map/ppermute | solution.py:559
  5.5 6.3 %collective-permute-start = (f32[24,4,456]{2,1,0:T(4,128)S(1)}, f32[24,4,456]{2,1,0:T(4,128)S(1)}, u32[]{:S(2)}, u32[]{:S(2)}) collective-permute-start(f32[24,4,456]{2,1,0:T(4,128)S(1)} %get-tuple-element.27), channel_id=1, source_target_pairs={{0,1},{2,3},{4,5},{6,7},{1,0},{3,2},{5,4},{7,6},{8,9},{10,11},{12,... | collective-permute-start | bytes 525320 | tf_op jit(solution)/shard_map/ppermute | solution.py:559
  5.6 1.1 %copy-start.1 = (f32[24,16,456]{2,1,0:T(8,128)S(1)}, f32[24,16,456]{2,1,0:T(8,128)}, u32[]{:S(2)}) copy-start(f32[24,16,456]{2,1,0:T(8,128)} %own_ref.1) | copy-start | bytes 2101252
  6.7 1.0 %copy-start.9 = (bf16[456,512]{1,0:T(8,128)(2,1)S(1)}, bf16[456,512]{1,0:T(8,128)(2,1)}, u32[]{:S(2)}) copy-start(bf16[456,512]{1,0:T(8,128)(2,1)} %constant.36.clone.rot_ref) | copy-start | bytes 1400836
  8.4 2.1 %copy-start = (f32[4,456,456]{2,1,0:T(8,128)S(1)}, f32[4,456,456]{2,1,0:T(8,128)}, u32[]{:S(2)}) copy-start(f32[4,456,456]{2,1,0:T(8,128)} %weight_ref.1) | copy-start | bytes 9980932
  11.0 6.7 %copy-start.2 = (f32[4,456,456]{2,1,0:T(8,128)S(1)}, f32[4,456,456]{2,1,0:T(8,128)}, u32[]{:S(2)}) copy-start(f32[4,456,456]{2,1,0:T(8,128)} %down_ref.1) | copy-start | bytes 9980932
  11.0 6.7 %copy-start.3 = (f32[456,456]{1,0:T(8,128)S(1)}, f32[456,456]{1,0:T(8,128)}, u32[]{:S(2)}) copy-start(f32[456,456]{1,0:T(8,128)} %inv_ref.1) | copy-start | bytes 2495236
  11.0 6.7 %copy-start.4 = (s32[24,16,40]{2,1,0:T(8,128)S(1)}, s32[24,16,40]{2,1,0:T(8,128)}, u32[]{:S(2)}) copy-start(s32[24,16,40]{2,1,0:T(8,128)} %llist_ref.1) | copy-start | bytes 184324
  11.0 6.7 %copy-start.6 = (s32[12,8,40]{2,1,0:T(8,128)S(1)}, s32[12,8,40]{2,1,0:T(8,128)}, u32[]{:S(2)}) copy-start(s32[12,8,40]{2,1,0:T(8,128)} %plist_ref.1) | copy-start | bytes 46084
  14.4 6.6 %collective-permute-start.2 = (f32[4,2,40,128]{3,2,1,0:T(8,128)S(1)}, f32[4,2,40,128]{3,2,1,0:T(8,128)S(1)}, u32[]{:S(2)}, u32[]{:S(2)}) collective-permute-start(f32[4,2,40,128]{3,2,1,0:T(8,128)S(1)} %get-tuple-element.17), channel_id=1, source_target_pairs={{0,8},{16,24},{8,0},{24,16},{1,9},{17,25},{9,1},{25,17},{2,10},{18... | collective-permute-start | bytes 491528 | tf_op jit(solution)/shard_map/ppermute | solution.py:559
  15.7 7.6 %collective-permute-start.3 = (f32[4,2,40,128]{3,2,1,0:T(8,128)S(1)}, f32[4,2,40,128]{3,2,1,0:T(8,128)S(1)}, u32[]{:S(2)}, u32[]{:S(2)}) collective-permute-start(f32[4,2,40,128]{3,2,1,0:T(8,128)S(1)} %get-tuple-element.18), channel_id=1, source_target_pairs={{8,16},{16,8},{9,17},{17,9},{10,18},{18,10},{11,19},{19,11},{12,20... | collective-permute-start | bytes 491528 | tf_op jit(solution)/shard_map/ppermute | solution.py:559
  17.7 5.7 %copy-start.5 = (f32[12,8,456]{2,1,0:T(8,128)S(1)}, f32[12,8,456]{2,1,0:T(8,128)}, u32[]{:S(2)}) copy-start(f32[12,8,456]{2,1,0:T(8,128)} %pin_ref.1) | copy-start | bytes 525316
  17.7 5.7 %copy-start.8 = (bf16[512,456]{1,0:T(8,128)(2,1)S(1)}, bf16[512,456]{1,0:T(8,128)(2,1)}, u32[]{:S(2)}) copy-start(bf16[512,456]{1,0:T(8,128)(2,1)} %constant.37.clone.back) | copy-start | bytes 1400836
  17.7 5.7 %copy-start.10 = (s32[108]{0:T(128)S(1)}, s32[108]{0:T(128)}, u32[]{:S(2)}) copy-start(s32[108]{0:T(128)} %constant.40.clone.pick_ref) | copy-start | bytes 1300
  17.7 5.7 %copy-start.11 = (s32[108]{0:T(128)S(1)}, s32[108]{0:T(128)}, u32[]{:S(2)}) copy-start(s32[108]{0:T(128)} %constant.39.clone.entry_ref) | copy-start | bytes 1300
  23.4 4.0 %copy-start.7 = (bf16[2,40,256,256]{3,2,1,0:T(8,128)(2,1)S(1)}, bf16[2,40,256,256]{3,2,1,0:T(8,128)(2,1)}, u32[]{:S(2)}) copy-start(bf16[2,40,256,256]{3,2,1,0:T(8,128)(2,1)} %constant.38.clone.table) | copy-start | bytes 31457284
